TPU v7x, 512 devices: a whole 4x8x8 slice. The times are simulated.
512 devices in a mesh: tm: 8 (over x, z_lo), lat: 64 (over z_hi, y, core).
Axes of the slice: x: 4, y: 8, z: 8 (z_hi: 4, z_lo: 2; z = z_hi * 2 + z_lo), core: 2. Of those that a mesh axis runs over, the one named last changes fastest.
Arguments:
- lam: float32 [8, 128, 216, 256], P('tm', 'lat'), may hold values from -6 to 6
- incr: float32 [8, 128, 216, 256], P('tm', 'lat'), may hold values from -6 to 6
- winds: float32 [8, 4, 128, 256], P('tm', None, 'lat'), may hold values from 0.02 to 0.2
- mixing: float32 [8, 216, 216], P('tm'), may hold values from -0.2 to 1
- spread: float32 [8, 128, 216, 256], P('tm', 'lat'), may hold values from 0.3 to 3
- vert_corr: float32 [216, 216], replicated, may hold values from -0.2 to 1
- members: bfloat16 [8, 128, 4, 216, 256], P('tm', 'lat'), may hold values from -6 to 6
Outputs:
- lam_out: float32 [8, 128, 216, 256], P('tm', 'lat')
- incr_out: float32 [8, 128, 216, 256], P('tm', 'lat')
All inputs are finite; a program needn't handle non-finite values.
Results may differ from a plain program's by a relative error of at most 0.0027.
Values may be sent and summed in bfloat16 or wider, within the bound.
A program may use at most 64 MiB of HBM per device.

v0:
```python
import jax
import jax.numpy as jnp
from jax import lax
from jax.sharding import PartitionSpec as P

STEPS = 2


def extended_2(block, sides, width):
    for axis, dim in sides:
        count = lax.axis_size(axis)
        forward = [(i, i + 1) for i in range(count - 1)]
        backward = [(target, source) for source, target in forward]
        low = lax.ppermute(
            lax.slice_in_dim(block, block.shape[dim] - width, None, axis=dim), axis, forward
        )
        high = lax.ppermute(lax.slice_in_dim(block, 0, width, axis=dim), axis, backward)
        block = jnp.concatenate([low, block, high], axis=dim)
    return block


def from_behind(value, axis, steps):
    count = lax.axis_size(axis)
    first, last = (max(0, -steps), min(count, count - steps))
    return lax.ppermute(value, axis, [(source, source + steps) for source in range(first, last)])


def smooth(extended):
    middle = extended[1:-1]
    return middle + 0.25 * (
        extended[2:] + extended[:-2] + jnp.roll(middle, -1, -1) + jnp.roll(middle, 1, -1)
    )


def clim_smooth(field_in):
    return smooth(extended_2(field_in, (("lat", 0),), 1))


def window(winds_ext, margin, offset, span_rows):
    start = margin + offset
    return tuple((winds_ext[place, start : start + span_rows][:, None, :] for place in range(4)))


def forward_step(extended, coeffs, mixer):
    north, south, east, west = coeffs
    middle = extended[1:-1]
    centre = 1.0 - north - south - east - west
    combined = centre * middle + north * extended[2:] + south * extended[:-2]
    combined = combined + east * jnp.roll(middle, -1, 2) + west * jnp.roll(middle, 1, 2)
    return jnp.einsum("ab,rbl->ral", mixer, combined, precision=lax.Precision.HIGHEST)


def adjoint_step(extended, coeffs, mixer):
    north, south, east, west = coeffs
    turned = jnp.einsum("ba,rbl->ral", mixer, extended, precision=lax.Precision.HIGHEST)
    centre = 1.0 - north[1:-1] - south[1:-1] - east[1:-1] - west[1:-1]
    middle = turned[1:-1]
    result = centre * middle + (north * turned)[:-2] + (south * turned)[2:]
    result = result + jnp.roll(east[1:-1] * middle, 1, 2) + jnp.roll(west[1:-1] * middle, -1, 2)
    return result


def per_device(lam, incr, winds, mixing, spread, vert_corr, members):
    band_rows = lam.shape[1]
    state_lam = lam[0]
    state_incr = incr[0]
    mixer = mixing[0]
    spread_now = spread[0]
    members_now = members[0]
    winds_ext = extended_2(winds[0], (("lat", 1),), STEPS)
    lam_next = from_behind(state_lam.astype(jnp.bfloat16), "tm", -1).astype(state_lam.dtype)
    propagated = state_incr
    for section in range(STEPS):
        extended = extended_2(propagated.astype(jnp.bfloat16), (("lat", 0),), 1).astype(
            propagated.dtype
        )
        propagated = forward_step(extended, window(winds_ext, STEPS, 0, band_rows), mixer)
    arrived = from_behind(propagated.astype(jnp.bfloat16), "tm", 1).astype(propagated.dtype)
    adjoint_state = lam_next
    for section in range(STEPS):
        extended = extended_2(adjoint_state, (("lat", 0),), 1)
        adjoint_state = adjoint_step(extended, window(winds_ext, STEPS, -1, band_rows + 2), mixer)
    scaled = spread_now * state_lam
    turned = jnp.einsum("ba,rbl->ral", vert_corr, scaled, precision=lax.Precision.HIGHEST)
    smoothed = clim_smooth(clim_smooth(turned))
    clim = spread_now * jnp.einsum(
        "ab,rbl->ral", vert_corr, smoothed, precision=lax.Precision.HIGHEST
    )
    perturb = members_now.astype(jnp.float32)
    divisor = members_now.shape[1] - 1
    weighted = perturb * state_lam[:, None]
    weighted_ext = extended_2(weighted, (("lat", 0),), 1)
    ens = jnp.sum(perturb * smooth(weighted_ext), axis=1) / divisor
    lam_result = 0.5 * clim + 0.5 * ens + state_incr - arrived
    incr_result = state_lam - adjoint_state
    return (lam_result[None], incr_result[None])


def solution(mesh):
    in_specs = (
        P("tm", "lat", None, None),
        P("tm", "lat", None, None),
        P("tm", None, "lat", None),
        P("tm", None, None),
        P("tm", "lat", None, None),
        P(),
        P("tm", "lat", None, None, None),
    )
    out_specs = (P("tm", "lat", None, None), P("tm", "lat", None, None))
    return jax.shard_map(
        per_device, mesh=mesh, in_specs=in_specs, out_specs=out_specs, check_vma=False
    )
```

profile of v0, /device:TPU:189, one launch (start us, length us, event | category | flops | bytes accessed | tf_op | source)
XLA Modules:
  0.0 107.9 jit_solution(16856511966739044149)
XLA Ops:
  0.7 2.7 %collective-permute-start.15 = (f32[4,2,256]{2,1,0:T(2,128)}, f32[4,2,256]{2,1,0:T(2,128)S(1)}, u32[]{:S(2)}, u32[]{:S(2)}) collective-permute-start(f32[4,2,256]{2,1,0:T(2,128)} %bitcast.91), channel_id=1, source_target_pairs={{1,0},{2,1},{3,2},{4,3},{5,4},{6,5},{7,6},{8,7},{9,8},{10,9},{11,1... | collective-permute-start | bytes 24584 | tf_op jit(solution)/shard_map/ppermute | solution.py:17
  3.4 7.2 %collective-permute-start.14 = (f32[4,2,256]{2,1,0:T(2,128)}, f32[4,2,256]{2,1,0:T(2,128)S(1)}, u32[]{:S(2)}, u32[]{:S(2)}) collective-permute-start(f32[4,2,256]{2,1,0:T(2,128)} %bitcast.92), channel_id=1, source_target_pairs={{0,1},{1,2},{2,3},{3,4},{4,5},{5,6},{6,7},{7,8},{8,9},{9,10},{10,1... | collective-permute-start | bytes 24584 | tf_op jit(solution)/shard_map/ppermute | solution.py:14
  10.6 1.8 %convolution_bitcast_fusion.3 = f32[2,216,256]{2,1,0:T(8,128)S(1)} fusion(f32[1,2,216,256]{3,2,1,0:T(8,128)} %param.11, f32[216,216]{1,0:T(8,128)} %param.12, f32[1,2,216,256]{3,2,1,0:T(8,128)} %param.7), kind=kOutput, calls=%fused_computation.13 | convolution fusion | flops 286765056 | bytes 1513728 | tf_op jit(solution)/shard_map/ba,rbl->ral/dot_general | solution.py:84
  12.5 1.9 %collective-permute-start.1 = (f32[1,216,256]{2,1,0:T(8,128)S(1)}, f32[1,216,256]{2,1,0:T(8,128)S(1)}, u32[]{:S(2)}, u32[]{:S(2)}) collective-permute-start(f32[1,216,256]{2,1,0:T(8,128)S(1)} %get-tuple-element.33), channel_id=1, source_target_pairs={{0,1},{1,2},{2,3},{3,4},{4,5},{5,6},{6,7},{7,8},{8,9},{9,10},{10,1... | collective-permute-start | bytes 663560 | tf_op jit(solution)/shard_map/ppermute | solution.py:14
  14.4 2.5 %collective-permute-start = (f32[1,216,256]{2,1,0:T(8,128)S(1)}, f32[1,216,256]{2,1,0:T(8,128)S(1)}, u32[]{:S(2)}, u32[]{:S(2)}) collective-permute-start(f32[1,216,256]{2,1,0:T(8,128)S(1)} %get-tuple-element.32), channel_id=1, source_target_pairs={{1,0},{2,1},{3,2},{4,3},{5,4},{6,5},{7,6},{8,7},{9,8},{10,9},{11,1... | collective-permute-start | bytes 663560 | tf_op jit(solution)/shard_map/ppermute | solution.py:17
  17.1 1.9 %collective-permute-start.7 = (bf16[1,216,256]{2,1,0:T(8,128)(2,1)S(1)}, bf16[1,216,256]{2,1,0:T(8,128)(2,1)S(1)}, u32[]{:S(2)}, u32[]{:S(2)}) collective-permute-start(bf16[1,216,256]{2,1,0:T(8,128)(2,1)S(1)} %get-tuple-element.39), channel_id=1, source_target_pairs={{1,0},{2,1},{3,2},{4,3},{5,4},{6,5},{7,6},{8,7},{9,8},{10,9},{11,1... | collective-permute-start | bytes 331784 | tf_op jit(solution)/shard_map/ppermute | solution.py:17
  19.0 0.1 fusion.117
  19.1 0.2 fusion.118
  19.3 0.1 convert_multiply_fusion.1
  19.5 0.1 fusion.108
  19.6 0.3 fusion.106
  19.9 0.6 fusion.107
  20.6 7.9 %collective-permute-start.6 = (bf16[1,216,256]{2,1,0:T(8,128)(2,1)S(1)}, bf16[1,216,256]{2,1,0:T(8,128)(2,1)S(1)}, u32[]{:S(2)}, u32[]{:S(2)}) collective-permute-start(bf16[1,216,256]{2,1,0:T(8,128)(2,1)S(1)} %get-tuple-element.38), channel_id=1, source_target_pairs={{0,1},{1,2},{2,3},{3,4},{4,5},{5,6},{6,7},{7,8},{8,9},{9,10},{10,1... | collective-permute-start | bytes 331784 | tf_op jit(solution)/shard_map/ppermute | solution.py:14
  28.4 1.9 %collective-permute-start.5 = (f32[1,4,216,256]{3,2,1,0:T(8,128)S(1)}, f32[1,4,216,256]{3,2,1,0:T(8,128)S(1)}, u32[]{:S(2)}, u32[]{:S(2)}) collective-permute-start(f32[1,4,216,256]{3,2,1,0:T(8,128)S(1)} %get-tuple-element.7), channel_id=1, source_target_pairs={{0,1},{1,2},{2,3},{3,4},{4,5},{5,6},{6,7},{7,8},{8,9},{9,10},{10,1... | collective-permute-start | bytes 2654216 | tf_op jit(solution)/shard_map/ppermute | solution.py:14
  30.4 2.4 %collective-permute-start.4 = (f32[1,4,216,256]{3,2,1,0:T(8,128)S(1)}, f32[1,4,216,256]{3,2,1,0:T(8,128)S(1)}, u32[]{:S(2)}, u32[]{:S(2)}) collective-permute-start(f32[1,4,216,256]{3,2,1,0:T(8,128)S(1)} %get-tuple-element.6), channel_id=1, source_target_pairs={{1,0},{2,1},{3,2},{4,3},{5,4},{6,5},{7,6},{8,7},{9,8},{10,9},{11,1... | collective-permute-start | bytes 2654216 | tf_op jit(solution)/shard_map/ppermute | solution.py:17
  32.8 4.0 %collective-permute-start.11 = (bf16[2,216,256]{2,1,0:T(8,128)(2,1)S(1)}, bf16[2,216,256]{2,1,0:T(8,128)(2,1)S(1)}, u32[]{:S(2)}, u32[]{:S(2)}) collective-permute-start(bf16[2,216,256]{2,1,0:T(8,128)(2,1)S(1)} %bitcast_convert_fusion.1), channel_id=1, source_target_pairs={{64,0},{128,64},{192,128},{256,192},{320,256},{384,320},{448,384},... | collective-permute-start | bytes 663560 | tf_op jit(solution)/shard_map/ppermute | solution.py:25
  37.0 0.2 fusion.112
  37.2 0.8 fusion.8
  38.1 2.2 %collective-permute-start.9 = (bf16[1,216,256]{2,1,0:T(8,128)(2,1)S(1)}, bf16[1,216,256]{2,1,0:T(8,128)(2,1)S(1)}, u32[]{:S(2)}, u32[]{:S(2)}) collective-permute-start(bf16[1,216,256]{2,1,0:T(8,128)(2,1)S(1)} %get-tuple-element.37), channel_id=1, source_target_pairs={{1,0},{2,1},{3,2},{4,3},{5,4},{6,5},{7,6},{8,7},{9,8},{10,9},{11,1... | collective-permute-start | bytes 331784 | tf_op jit(solution)/shard_map/ppermute | solution.py:17
  40.3 7.6 %collective-permute-start.8 = (bf16[1,216,256]{2,1,0:T(8,128)(2,1)S(1)}, bf16[1,216,256]{2,1,0:T(8,128)(2,1)S(1)}, u32[]{:S(2)}, u32[]{:S(2)}) collective-permute-start(bf16[1,216,256]{2,1,0:T(8,128)(2,1)S(1)} %get-tuple-element.36), channel_id=1, source_target_pairs={{0,1},{1,2},{2,3},{3,4},{4,5},{5,6},{6,7},{7,8},{8,9},{9,10},{10,1... | collective-permute-start | bytes 331784 | tf_op jit(solution)/shard_map/ppermute | solution.py:14
  47.9 0.3 fusion.66
  48.1 0.2 fusion.115
  48.3 10.0 %collective-permute-done.9 = bf16[1,216,256]{2,1,0:T(8,128)(2,1)S(1)} collective-permute-done((bf16[1,216,256]{2,1,0:T(8,128)(2,1)S(1)}, bf16[1,216,256]{2,1,0:T(8,128)(2,1)S(1)}, u32[]{:S(2)}, u32[]{:S(2)}) %collective-permute-start.9) | collective-permute-done | bytes 110624 | tf_op jit(solution)/shard_map/ppermute | solution.py:17
  58.4 0.2 fusion.110
  58.6 0.1 fusion.109
  58.7 3.0 %collective-permute-done.11 = bf16[2,216,256]{2,1,0:T(8,128)(2,1)S(1)} collective-permute-done((bf16[2,216,256]{2,1,0:T(8,128)(2,1)S(1)}, bf16[2,216,256]{2,1,0:T(8,128)(2,1)S(1)}, u32[]{:S(2)}, u32[]{:S(2)}) %collective-permute-start.11) | collective-permute-done | bytes 221216 | tf_op jit(solution)/shard_map/ppermute | solution.py:25
  61.8 2.4 %collective-permute-start.13 = (f32[1,216,256]{2,1,0:T(8,128)S(1)}, f32[1,216,256]{2,1,0:T(8,128)S(1)}, u32[]{:S(2)}, u32[]{:S(2)}) collective-permute-start(f32[1,216,256]{2,1,0:T(8,128)S(1)} %get-tuple-element.35), channel_id=1, source_target_pairs={{1,0},{2,1},{3,2},{4,3},{5,4},{6,5},{7,6},{8,7},{9,8},{10,9},{11,1... | collective-permute-start | bytes 663560 | tf_op jit(solution)/shard_map/ppermute | solution.py:17
  64.2 7.4 %collective-permute-start.12 = (f32[1,216,256]{2,1,0:T(8,128)S(1)}, f32[1,216,256]{2,1,0:T(8,128)S(1)}, u32[]{:S(2)}, u32[]{:S(2)}) collective-permute-start(f32[1,216,256]{2,1,0:T(8,128)S(1)} %get-tuple-element.34), channel_id=1, source_target_pairs={{0,1},{1,2},{2,3},{3,4},{4,5},{5,6},{6,7},{7,8},{8,9},{9,10},{10,1... | collective-permute-start | bytes 663560 | tf_op jit(solution)/shard_map/ppermute | solution.py:14
  71.6 0.8 fusion.9
  72.5 2.2 %collective-permute-done.13 = f32[1,216,256]{2,1,0:T(8,128)S(1)} collective-permute-done((f32[1,216,256]{2,1,0:T(8,128)S(1)}, f32[1,216,256]{2,1,0:T(8,128)S(1)}, u32[]{:S(2)}, u32[]{:S(2)}) %collective-permute-start.13) | collective-permute-done | bytes 221216 | tf_op jit(solution)/shard_map/ppermute | solution.py:17
  74.7 1.0 convolution_bitcast_fusion.1
  75.8 0.2 slice.373
  75.9 0.1 slice.371
  76.1 0.3 fusion.28
  76.4 1.9 %collective-permute-start.17 = (f32[1,216,256]{2,1,0:T(8,128)S(1)}, f32[1,216,256]{2,1,0:T(8,128)S(1)}, u32[]{:S(2)}, u32[]{:S(2)}) collective-permute-start(f32[1,216,256]{2,1,0:T(8,128)S(1)} %get-tuple-element.21), channel_id=1, source_target_pairs={{1,0},{2,1},{3,2},{4,3},{5,4},{6,5},{7,6},{8,7},{9,8},{10,9},{11,1... | collective-permute-start | bytes 663560 | tf_op jit(solution)/shard_map/ppermute | solution.py:17
  78.3 10.6 %collective-permute-start.16 = (f32[1,216,256]{2,1,0:T(8,128)S(1)}, f32[1,216,256]{2,1,0:T(8,128)S(1)}, u32[]{:S(2)}, u32[]{:S(2)}) collective-permute-start(f32[1,216,256]{2,1,0:T(8,128)S(1)} %get-tuple-element.20), channel_id=1, source_target_pairs={{0,1},{1,2},{2,3},{3,4},{4,5},{5,6},{6,7},{7,8},{8,9},{9,10},{10,1... | collective-permute-start | bytes 663560 | tf_op jit(solution)/shard_map/ppermute | solution.py:14
  89.1 2.4 %collective-permute-start.3 = (f32[1,216,256]{2,1,0:T(8,128)S(1)}, f32[1,216,256]{2,1,0:T(8,128)S(1)}, u32[]{:S(2)}, u32[]{:S(2)}) collective-permute-start(f32[1,216,256]{2,1,0:T(8,128)S(1)} %get-tuple-element.27), channel_id=1, source_target_pairs={{0,1},{1,2},{2,3},{3,4},{4,5},{5,6},{6,7},{7,8},{8,9},{9,10},{10,1... | collective-permute-start | bytes 663560 | tf_op jit(solution)/shard_map/ppermute | solution.py:14
  91.5 1.1 %collective-permute-done.17 = f32[1,216,256]{2,1,0:T(8,128)S(1)} collective-permute-done((f32[1,216,256]{2,1,0:T(8,128)S(1)}, f32[1,216,256]{2,1,0:T(8,128)S(1)}, u32[]{:S(2)}, u32[]{:S(2)}) %collective-permute-start.17) | collective-permute-done | bytes 221216 | tf_op jit(solution)/shard_map/ppermute | solution.py:17
  92.6 1.9 %collective-permute-start.2 = (f32[1,216,256]{2,1,0:T(8,128)S(1)}, f32[1,216,256]{2,1,0:T(8,128)S(1)}, u32[]{:S(2)}, u32[]{:S(2)}) collective-permute-start(f32[1,216,256]{2,1,0:T(8,128)S(1)} %get-tuple-element.26), channel_id=1, source_target_pairs={{1,0},{2,1},{3,2},{4,3},{5,4},{6,5},{7,6},{8,7},{9,8},{10,9},{11,1... | collective-permute-start | bytes 663560 | tf_op jit(solution)/shard_map/ppermute | solution.py:17
  94.5 2.7 %collective-permute-start.10 = (bf16[2,216,256]{2,1,0:T(8,128)(2,1)S(1)}, bf16[2,216,256]{2,1,0:T(8,128)(2,1)S(1)}, u32[]{:S(2)}, u32[]{:S(2)}) collective-permute-start(bf16[2,216,256]{2,1,0:T(8,128)(2,1)S(1)} %fusion.9), channel_id=1, source_target_pairs={{0,64},{64,128},{128,192},{192,256},{256,320},{320,384},{384,448},... | collective-permute-start | bytes 663560 | tf_op jit(solution)/shard_map/ppermute | solution.py:25
  97.2 1.0 convolution_bitcast_fusion
  98.3 0.2 slice.384
  98.5 0.1 slice.382
  98.6 1.1 fusion.24
  99.7 0.9 fusion
  100.6 4.7 %collective-permute-done.2 = f32[1,216,256]{2,1,0:T(8,128)S(1)} collective-permute-done((f32[1,216,256]{2,1,0:T(8,128)S(1)}, f32[1,216,256]{2,1,0:T(8,128)S(1)}, u32[]{:S(2)}, u32[]{:S(2)}) %collective-permute-start.2) | collective-permute-done | bytes 221216 | tf_op jit(solution)/shard_map/ppermute | solution.py:17
  105.3 0.9 collective-permute-done.10
  106.2 1.6 %fusion.57 = f32[1,2,216,256]{3,2,1,0:T(8,128)} fusion(f32[2,216,256]{2,1,0:T(8,128)S(1)} %fusion.66, f32[1,216,256]{2,1,0:T(8,128)S(1)} %collective-permute-done.3, f32[1,216,256]{2,1,0:T(8,128)S(1)} %collective-permute-done.2, f32[2,216,1]{2,1,0:T(8,128)S(1)} %get-tuple-element.23, f32[2,216,255]{2,1,0:T(8,128)S(1)} %get-tuple-element.25, ...), kind=kOutput, calls=%fused_computation.67 | convolution fusion | flops 288423936 | bytes 3946752 | tf_op jit(solution)/shard_map/ab,rbl->ral/dot_general | solution.py:86
  (48 shorter events, 0.9 us)
Async XLA Ops:
  0.6 36.6 %copy-start = (f32[1,216,216]{2,1,0:T(8,128)S(1)}, f32[1,216,216]{2,1,0:T(8,128)}, u32[]{:S(2)}) copy-start(f32[1,216,216]{2,1,0:T(8,128)} %param.10) | copy-start | bytes 559876
  0.6 16.3 %copy-start.4 = (f32[1,2,216,256]{3,2,1,0:T(8,128)S(1)}, f32[1,2,216,256]{3,2,1,0:T(8,128)}, u32[]{:S(2)}) copy-start(f32[1,2,216,256]{3,2,1,0:T(8,128)} %param.8) | copy-start | bytes 1327108
  0.7 19.9 %collective-permute-start.15 = (f32[4,2,256]{2,1,0:T(2,128)}, f32[4,2,256]{2,1,0:T(2,128)S(1)}, u32[]{:S(2)}, u32[]{:S(2)}) collective-permute-start(f32[4,2,256]{2,1,0:T(2,128)} %bitcast.91), channel_id=1, source_target_pairs={{1,0},{2,1},{3,2},{4,3},{5,4},{6,5},{7,6},{8,7},{9,8},{10,9},{11,1... | collective-permute-start | bytes 24584 | tf_op jit(solution)/shard_map/ppermute | solution.py:17
  3.4 25.1 %collective-permute-start.14 = (f32[4,2,256]{2,1,0:T(2,128)}, f32[4,2,256]{2,1,0:T(2,128)S(1)}, u32[]{:S(2)}, u32[]{:S(2)}) collective-permute-start(f32[4,2,256]{2,1,0:T(2,128)} %bitcast.92), channel_id=1, source_target_pairs={{0,1},{1,2},{2,3},{3,4},{4,5},{5,6},{6,7},{7,8},{8,9},{9,10},{10,1... | collective-permute-start | bytes 24584 | tf_op jit(solution)/shard_map/ppermute | solution.py:14
  12.5 25.6 %collective-permute-start.1 = (f32[1,216,256]{2,1,0:T(8,128)S(1)}, f32[1,216,256]{2,1,0:T(8,128)S(1)}, u32[]{:S(2)}, u32[]{:S(2)}) collective-permute-start(f32[1,216,256]{2,1,0:T(8,128)S(1)} %get-tuple-element.33), channel_id=1, source_target_pairs={{0,1},{1,2},{2,3},{3,4},{4,5},{5,6},{6,7},{7,8},{8,9},{9,10},{10,1... | collective-permute-start | bytes 663560 | tf_op jit(solution)/shard_map/ppermute | solution.py:14
  14.4 4.9 %copy-start.6 = (f32[1,4,2,256]{3,2,1,0:T(2,128)S(1)}, f32[1,4,2,256]{3,2,1,0:T(2,128)}, u32[]{:S(2)}) copy-start(f32[1,4,2,256]{3,2,1,0:T(2,128)} %param.9) | copy-start | bytes 24580
  14.4 4.9 %copy-start.1 = (f32[1,2,216,256]{3,2,1,0:T(8,128)S(1)}, f32[1,2,216,256]{3,2,1,0:T(8,128)}, u32[]{:S(2)}) copy-start(f32[1,2,216,256]{3,2,1,0:T(8,128)} %param.7) | copy-start | bytes 1327108
  14.4 4.9 %copy-start.2 = (bf16[1,2,4,216,256]{4,3,2,1,0:T(8,128)(2,1)S(1)}, bf16[1,2,4,216,256]{4,3,2,1,0:T(8,128)(2,1)}, u32[]{:S(2)}) copy-start(bf16[1,2,4,216,256]{4,3,2,1,0:T(8,128)(2,1)} %param.13) | copy-start | bytes 2654212
  14.4 25.8 %collective-permute-start = (f32[1,216,256]{2,1,0:T(8,128)S(1)}, f32[1,216,256]{2,1,0:T(8,128)S(1)}, u32[]{:S(2)}, u32[]{:S(2)}) collective-permute-start(f32[1,216,256]{2,1,0:T(8,128)S(1)} %get-tuple-element.32), channel_id=1, source_target_pairs={{1,0},{2,1},{3,2},{4,3},{5,4},{6,5},{7,6},{8,7},{9,8},{10,9},{11,1... | collective-permute-start | bytes 663560 | tf_op jit(solution)/shard_map/ppermute | solution.py:17
  17.1 13.4 %collective-permute-start.7 = (bf16[1,216,256]{2,1,0:T(8,128)(2,1)S(1)}, bf16[1,216,256]{2,1,0:T(8,128)(2,1)S(1)}, u32[]{:S(2)}, u32[]{:S(2)}) collective-permute-start(bf16[1,216,256]{2,1,0:T(8,128)(2,1)S(1)} %get-tuple-element.39), channel_id=1, source_target_pairs={{1,0},{2,1},{3,2},{4,3},{5,4},{6,5},{7,6},{8,7},{9,8},{10,9},{11,1... | collective-permute-start | bytes 331784 | tf_op jit(solution)/shard_map/ppermute | solution.py:17
  20.6 12.3 %collective-permute-start.6 = (bf16[1,216,256]{2,1,0:T(8,128)(2,1)S(1)}, bf16[1,216,256]{2,1,0:T(8,128)(2,1)S(1)}, u32[]{:S(2)}, u32[]{:S(2)}) collective-permute-start(bf16[1,216,256]{2,1,0:T(8,128)(2,1)S(1)} %get-tuple-element.38), channel_id=1, source_target_pairs={{0,1},{1,2},{2,3},{3,4},{4,5},{5,6},{6,7},{7,8},{8,9},{9,10},{10,1... | collective-permute-start | bytes 331784 | tf_op jit(solution)/shard_map/ppermute | solution.py:14
  28.4 71.2 %collective-permute-start.5 = (f32[1,4,216,256]{3,2,1,0:T(8,128)S(1)}, f32[1,4,216,256]{3,2,1,0:T(8,128)S(1)}, u32[]{:S(2)}, u32[]{:S(2)}) collective-permute-start(f32[1,4,216,256]{3,2,1,0:T(8,128)S(1)} %get-tuple-element.7), channel_id=1, source_target_pairs={{0,1},{1,2},{2,3},{3,4},{4,5},{5,6},{6,7},{7,8},{8,9},{9,10},{10,1... | collective-permute-start | bytes 2654216 | tf_op jit(solution)/shard_map/ppermute | solution.py:14
  30.4 69.2 %collective-permute-start.4 = (f32[1,4,216,256]{3,2,1,0:T(8,128)S(1)}, f32[1,4,216,256]{3,2,1,0:T(8,128)S(1)}, u32[]{:S(2)}, u32[]{:S(2)}) collective-permute-start(f32[1,4,216,256]{3,2,1,0:T(8,128)S(1)} %get-tuple-element.6), channel_id=1, source_target_pairs={{1,0},{2,1},{3,2},{4,3},{5,4},{6,5},{7,6},{8,7},{9,8},{10,9},{11,1... | collective-permute-start | bytes 2654216 | tf_op jit(solution)/shard_map/ppermute | solution.py:17
  32.8 28.9 %collective-permute-start.11 = (bf16[2,216,256]{2,1,0:T(8,128)(2,1)S(1)}, bf16[2,216,256]{2,1,0:T(8,128)(2,1)S(1)}, u32[]{:S(2)}, u32[]{:S(2)}) collective-permute-start(bf16[2,216,256]{2,1,0:T(8,128)(2,1)S(1)} %bitcast_convert_fusion.1), channel_id=1, source_target_pairs={{64,0},{128,64},{192,128},{256,192},{320,256},{384,320},{448,384},... | collective-permute-start | bytes 663560 | tf_op jit(solution)/shard_map/ppermute | solution.py:25
  38.1 20.3 %collective-permute-start.9 = (bf16[1,216,256]{2,1,0:T(8,128)(2,1)S(1)}, bf16[1,216,256]{2,1,0:T(8,128)(2,1)S(1)}, u32[]{:S(2)}, u32[]{:S(2)}) collective-permute-start(bf16[1,216,256]{2,1,0:T(8,128)(2,1)S(1)} %get-tuple-element.37), channel_id=1, source_target_pairs={{1,0},{2,1},{3,2},{4,3},{5,4},{6,5},{7,6},{8,7},{9,8},{10,9},{11,1... | collective-permute-start | bytes 331784 | tf_op jit(solution)/shard_map/ppermute | solution.py:17
  40.3 18.1 %collective-permute-start.8 = (bf16[1,216,256]{2,1,0:T(8,128)(2,1)S(1)}, bf16[1,216,256]{2,1,0:T(8,128)(2,1)S(1)}, u32[]{:S(2)}, u32[]{:S(2)}) collective-permute-start(bf16[1,216,256]{2,1,0:T(8,128)(2,1)S(1)} %get-tuple-element.36), channel_id=1, source_target_pairs={{0,1},{1,2},{2,3},{3,4},{4,5},{5,6},{6,7},{7,8},{8,9},{9,10},{10,1... | collective-permute-start | bytes 331784 | tf_op jit(solution)/shard_map/ppermute | solution.py:14
  61.8 12.9 %collective-permute-start.13 = (f32[1,216,256]{2,1,0:T(8,128)S(1)}, f32[1,216,256]{2,1,0:T(8,128)S(1)}, u32[]{:S(2)}, u32[]{:S(2)}) collective-permute-start(f32[1,216,256]{2,1,0:T(8,128)S(1)} %get-tuple-element.35), channel_id=1, source_target_pairs={{1,0},{2,1},{3,2},{4,3},{5,4},{6,5},{7,6},{8,7},{9,8},{10,9},{11,1... | collective-permute-start | bytes 663560 | tf_op jit(solution)/shard_map/ppermute | solution.py:17
  64.2 10.4 %collective-permute-start.12 = (f32[1,216,256]{2,1,0:T(8,128)S(1)}, f32[1,216,256]{2,1,0:T(8,128)S(1)}, u32[]{:S(2)}, u32[]{:S(2)}) collective-permute-start(f32[1,216,256]{2,1,0:T(8,128)S(1)} %get-tuple-element.34), channel_id=1, source_target_pairs={{0,1},{1,2},{2,3},{3,4},{4,5},{5,6},{6,7},{7,8},{8,9},{9,10},{10,1... | collective-permute-start | bytes 663560 | tf_op jit(solution)/shard_map/ppermute | solution.py:14
  76.4 16.2 %collective-permute-start.17 = (f32[1,216,256]{2,1,0:T(8,128)S(1)}, f32[1,216,256]{2,1,0:T(8,128)S(1)}, u32[]{:S(2)}, u32[]{:S(2)}) collective-permute-start(f32[1,216,256]{2,1,0:T(8,128)S(1)} %get-tuple-element.21), channel_id=1, source_target_pairs={{1,0},{2,1},{3,2},{4,3},{5,4},{6,5},{7,6},{8,7},{9,8},{10,9},{11,1... | collective-permute-start | bytes 663560 | tf_op jit(solution)/shard_map/ppermute | solution.py:17
  78.3 16.2 %collective-permute-start.16 = (f32[1,216,256]{2,1,0:T(8,128)S(1)}, f32[1,216,256]{2,1,0:T(8,128)S(1)}, u32[]{:S(2)}, u32[]{:S(2)}) collective-permute-start(f32[1,216,256]{2,1,0:T(8,128)S(1)} %get-tuple-element.20), channel_id=1, source_target_pairs={{0,1},{1,2},{2,3},{3,4},{4,5},{5,6},{6,7},{7,8},{8,9},{9,10},{10,1... | collective-permute-start | bytes 663560 | tf_op jit(solution)/shard_map/ppermute | solution.py:14
  89.1 11.5 %collective-permute-start.3 = (f32[1,216,256]{2,1,0:T(8,128)S(1)}, f32[1,216,256]{2,1,0:T(8,128)S(1)}, u32[]{:S(2)}, u32[]{:S(2)}) collective-permute-start(f32[1,216,256]{2,1,0:T(8,128)S(1)} %get-tuple-element.27), channel_id=1, source_target_pairs={{0,1},{1,2},{2,3},{3,4},{4,5},{5,6},{6,7},{7,8},{8,9},{9,10},{10,1... | collective-permute-start | bytes 663560 | tf_op jit(solution)/shard_map/ppermute | solution.py:14
  92.6 12.7 %collective-permute-start.2 = (f32[1,216,256]{2,1,0:T(8,128)S(1)}, f32[1,216,256]{2,1,0:T(8,128)S(1)}, u32[]{:S(2)}, u32[]{:S(2)}) collective-permute-start(f32[1,216,256]{2,1,0:T(8,128)S(1)} %get-tuple-element.26), channel_id=1, source_target_pairs={{1,0},{2,1},{3,2},{4,3},{5,4},{6,5},{7,6},{8,7},{9,8},{10,9},{11,1... | collective-permute-start | bytes 663560 | tf_op jit(solution)/shard_map/ppermute | solution.py:17
  94.5 11.7 %collective-permute-start.10 = (bf16[2,216,256]{2,1,0:T(8,128)(2,1)S(1)}, bf16[2,216,256]{2,1,0:T(8,128)(2,1)S(1)}, u32[]{:S(2)}, u32[]{:S(2)}) collective-permute-start(bf16[2,216,256]{2,1,0:T(8,128)(2,1)S(1)} %fusion.9), channel_id=1, source_target_pairs={{0,64},{64,128},{128,192},{192,256},{256,320},{320,384},{384,448},... | collective-permute-start | bytes 663560 | tf_op jit(solution)/shard_map/ppermute | solution.py:25
  99.7 6.6 %copy-start.3 = (f32[1,2,216,256]{3,2,1,0:T(8,128)S(1)}, f32[1,2,216,256]{3,2,1,0:T(8,128)}, u32[]{:S(2)}) copy-start(f32[1,2,216,256]{3,2,1,0:T(8,128)} %param.11) | copy-start | bytes 1327108
  99.7 6.6 %copy-start.5 = (f32[216,216]{1,0:T(8,128)S(1)}, f32[216,216]{1,0:T(8,128)}, u32[]{:S(2)}) copy-start(f32[216,216]{1,0:T(8,128)} %param.12) | copy-start | bytes 559876
where the time goes:
time: 108 us
  starting transfers between devices  71.6 us (66%)
  waiting for transfers between devices  22 us (20%)
  matrix products  6.99 us (6%)
  other arithmetic  3.04 us (3%)
  local copies, waits for them, and re-layouts  3.02 us (3%)
  between operations  1.22 us (1%)
    ppermute x8, starting transfers between devices, extended_2(): lax.ppermute(lax.slice_in_dim(block, block.shape[dim] - width, None, axis...  46.9 us
    ppermute x8, waiting for transfers between devices, extended_2(): lax.ppermute(lax.slice_in_dim(block, 0, width, axis=dim), axis, backward)  18 us
    ppermute x8, starting transfers between devices, extended_2(): lax.ppermute(lax.slice_in_dim(block, 0, width, axis=dim), axis, backward)  18 us
    ppermute x2, starting transfers between devices, from_behind(): lax.ppermute(value, axis, [(source, source + steps) for source in range(f...  6.67 us
    ppermute x2, waiting for transfers between devices, from_behind(): lax.ppermute(value, axis, [(source, source + steps) for source in range(f...  3.96 us
  transfers between devices with their start and end apart: 18, of which 6 were waited for; matrix products, arithmetic and copies ran while one was open for 11% of the time, Pallas kernels for 0%

commit v1 on v0

v1 whole, which is shorter than its diff:
```python
import jax
import jax.numpy as jnp
from jax import lax
from jax.experimental import pallas as pl
from jax.experimental.pallas import tpu as pltpu
from jax.sharding import PartitionSpec as P

MESH = pl.DeviceIdType.MESH
F32, BF16 = jnp.float32, jnp.bfloat16
COMP, LON, NENS = 216, 256, 4
TM, LAT, BAND = 8, 64, 16
CHUNKS = [(at, min(32, COMP - at)) for at in range(0, COMP, 32)]

WIN, INC, SCA, LNX, QEN = 0, 1, 3, 5, 7
ITEMS = 11
ROUTED = (SCA, SCA + 1, QEN + 1, QEN + 2, QEN + 3)


def split(value):
    high = value.astype(BF16)
    return high, (value - high.astype(F32)).astype(BF16)


def dot(a, b):
    return jnp.dot(a, b, preferred_element_type=F32)


def product(mats, base, value):
    high, low = split(value)
    return dot(mats[base], high) + (dot(mats[base + 1], high) + dot(mats[base], low))


def product_16(mats, base, value):
    return dot(mats[base], value) + dot(mats[base + 1], value)


def east_of(value):
    return pltpu.roll(value, LON - 1, 1)


def west_of(value):
    return pltpu.roll(value, 1, 1)


def kernel(
    lam, incr, winds, mixing, spread, vert, members, lam_out, incr_out,
    i6, l6, s6, w3, q_send, q_recv, lam_send, prop_send, arrived, fwd,
    mats, scaled, za, zb, ens,
    tm_send, tm_recv, up_send, up_recv, dn_send, dn_recv, f_in, f_out,
):
    tm, lat = lax.axis_index("tm"), lax.axis_index("lat")
    place = lax.rem(lat, BAND)
    has_up, has_dn = lat < LAT - 1, lat > 0
    has_next, has_prev = tm < TM - 1, tm > 0
    cross_up = (place == BAND - 1) & has_up
    cross_dn = (place == 0) & has_dn
    fwd_up = (place == BAND - 2) & (lat >= BAND)
    fwd_dn = (place == 1) & (lat < LAT - BAND)

    barrier = pltpu.get_barrier_semaphore()
    greetings = (
        (has_next, {"tm": tm + 1}),
        (has_prev, {"tm": tm - 1}),
        (has_up, {"lat": lat + 1}),
        (has_dn, {"lat": lat - 1}),
        (cross_up, {"lat": lat - (BAND - 2)}),
        (cross_dn, {"lat": lat + (BAND - 2)}),
        (fwd_up, {"lat": lat - (BAND - 1)}),
        (fwd_dn, {"lat": lat + (BAND - 1)}),
    )
    targets = 0
    for cond, where in greetings:
        targets = targets + jnp.where(cond, 1, 0)

        @pl.when(cond)
        def _():
            pl.semaphore_signal(barrier, inc=1, device_id=where, device_id_type=MESH)

    def ends(item, up):
        if item == WIN:
            return w3.at[1], w3.at[0 if up else 2]
        for first, buffer in ((INC, i6), (SCA, s6), (LNX, l6)):
            if first <= item < first + 2:
                row = item - first
                return buffer.at[2 + row], buffer.at[row if up else 4 + row]
        m = item - QEN
        return q_send.at[1 if up else 0, m], q_recv.at[0 if up else 1, m]

    def to_lat(item, up):
        src, dst = ends(item, up)
        send, recv = (up_send, up_recv) if up else (dn_send, dn_recv)
        where = {"lat": lat + 1 if up else lat - 1}
        return pltpu.make_async_remote_copy(
            src, dst, send.at[item], recv.at[item], device_id=where, device_id_type=MESH
        )

    def to_fwd(item, up):
        src, _ = ends(item, up)
        at = ROUTED.index(item)
        send = up_send if up else dn_send
        where = {"lat": lat + (BAND - 1) if up else lat - (BAND - 1)}
        return pltpu.make_async_remote_copy(
            src, fwd.at[at], send.at[item], f_in.at[at], device_id=where, device_id_type=MESH
        )

    def from_fwd(item, up):
        _, dst = ends(item, up)
        at = ROUTED.index(item)
        recv = up_recv if up else dn_recv
        where = {"lat": lat - (BAND - 2) if up else lat + (BAND - 2)}
        return pltpu.make_async_remote_copy(
            fwd.at[at], dst, f_out.at[at], recv.at[item], device_id=where, device_id_type=MESH
        )

    def start_lat(items, cond=True):
        for up, has, cross in ((True, has_up, cross_up), (False, has_dn, cross_dn)):
            plain = [item for item in items if item not in ROUTED]
            routed = [item for item in items if item in ROUTED]

            @pl.when(has & cond)
            def _():
                for item in plain:
                    to_lat(item, up).start()

            if routed:

                @pl.when(has & jnp.logical_not(cross) & cond)
                def _():
                    for item in routed:
                        to_lat(item, up).start()

                @pl.when(cross & cond)
                def _():
                    for item in routed:
                        to_fwd(item, up).start()

    def pass_on(items):
        for up, cond in ((True, fwd_up), (False, fwd_dn)):

            @pl.when(cond)
            def _():
                for item in items:
                    copy = from_fwd(item, up)
                    pltpu.make_async_remote_copy(
                        fwd.at[ROUTED.index(item)],
                        fwd.at[ROUTED.index(item)],
                        f_out.at[ROUTED.index(item)],
                        f_in.at[ROUTED.index(item)],
                        device_id={"lat": lat - 1 if up else lat + 1},
                        device_id_type=MESH,
                    ).wait_recv()
                    copy.start()

    def await_lat(items, cond=True):
        for up, has in ((True, has_dn), (False, has_up)):

            @pl.when(has & cond)
            def _():
                for item in items:
                    to_lat(item, up).wait_recv()

    def dual_to_prev(row):
        return pltpu.make_async_remote_copy(
            lam_send.at[row], l6.at[2 + row], tm_send.at[row], tm_recv.at[row],
            device_id={"tm": tm - 1}, device_id_type=MESH,
        )

    def prop_to_next(row):
        return pltpu.make_async_remote_copy(
            prop_send.at[row], arrived.at[row], tm_send.at[2 + row], tm_recv.at[2 + row],
            device_id={"tm": tm + 1}, device_id_type=MESH,
        )

    w3[1] = winds[...]
    for row in range(2):
        for at, size in CHUNKS:
            rows = pl.ds(at, size)
            dual = lam[row, rows, :]
            product_now = spread[row, rows, :] * dual
            lam_send[row, rows, :] = dual.astype(BF16)
            i6[2 + row, rows, :] = incr[row, rows, :].astype(BF16)
            scaled[row, rows, :] = product_now
            s6[2 + row, rows, :] = product_now.astype(BF16)

    @pl.when(jnp.logical_not(has_dn))
    def _():
        w3[0] = jnp.zeros_like(w3[0])
        for buffer in (i6, l6, s6):
            for row in (0, 1):
                buffer[row] = jnp.zeros_like(buffer[row])
        for m in range(NENS):
            q_recv[0, m] = jnp.zeros_like(q_recv[0, m])

    @pl.when(jnp.logical_not(has_up))
    def _():
        w3[2] = jnp.zeros_like(w3[2])
        for buffer in (i6, l6, s6):
            for row in (4, 5):
                buffer[row] = jnp.zeros_like(buffer[row])
        for m in range(NENS):
            q_recv[1, m] = jnp.zeros_like(q_recv[1, m])

    @pl.when(jnp.logical_not(has_prev))
    def _():
        arrived[...] = jnp.zeros_like(arrived)

    pl.semaphore_wait(barrier, targets)

    @pl.when(has_prev)
    def _():
        dual_to_prev(0).start()
        dual_to_prev(1).start()

    start_lat([WIN, INC, INC + 1], has_next)
    start_lat([SCA, SCA + 1])

    for base, matrix in ((0, mixing[...]), (4, vert[...])):
        mats[base], mats[base + 1] = split(matrix)
        mats[base + 2], mats[base + 3] = split(matrix.T)

    for at, size in CHUNKS:
        rows = pl.ds(at, size)
        totals = [None, None]
        duals = [lam[row, rows, :] for row in range(2)]
        for m in range(NENS):
            perturb = [members[row, m, rows, :].astype(F32) for row in range(2)]
            weighted = [perturb[row] * duals[row] for row in range(2)]
            for row in range(2):
                q_send[row, m, rows, :] = weighted[row].astype(BF16)
                near = weighted[1 - row] + east_of(weighted[row]) + west_of(weighted[row])
                term = perturb[row] * (weighted[row] + 0.25 * near)
                totals[row] = term if m == 0 else totals[row] + term
        for row in range(2):
            ens[row, rows, :] = totals[row]

    def weights(i):
        block, row = (i + 2) // 2, (i + 2) % 2
        north, south, east, west = (w3[block, 2 * p + row : 2 * p + row + 1, :] for p in range(4))
        return north, south, east, west, 1.0 - north - south - east - west

    low_edge = jnp.where(has_dn, 1.0, 0.0).astype(F32)
    high_edge = jnp.where(has_up, 1.0, 0.0).astype(F32)

    def inside(i, value):
        if i == -1:
            return value * low_edge
        if i == 2:
            return value * high_edge
        return value

    @pl.when(has_next)
    def _():
        await_lat([WIN, INC, INC + 1])

        def transport(of, i, rows):
            north, south, east, west, centre = weights(i)
            here = of(i, rows)
            total = centre * here + north * of(i + 1, rows) + south * of(i - 1, rows)
            return total + east * east_of(here) + west * west_of(here)

        def first(i, rows):
            if 0 <= i < 2:
                return incr[i, rows, :]
            return i6[i + 2, rows, :].astype(F32)

        for i in range(-1, 3):
            for at, size in CHUNKS:
                rows = pl.ds(at, size)
                za[i + 1, rows, :] = inside(i, transport(first, i, rows))
        for i in range(4):
            zb[i] = product(mats, 0, za[i])
        for i in range(2):
            for at, size in CHUNKS:
                rows = pl.ds(at, size)
                za[i, rows, :] = transport(lambda j, r: zb[j + 1, r, :], i, rows)
        for i in range(2):
            prop_send[i] = product(mats, 0, za[i]).astype(BF16)
            prop_to_next(i).start()

    for row in range(2):

        @pl.when(has_next)
        def _():
            dual_to_prev(row).wait_recv()

        start_lat([LNX + row], has_next)

    start_lat([QEN + m for m in range(NENS)])

    pass_on([SCA, SCA + 1])
    await_lat([SCA, SCA + 1])

    def smooth(of, i, rows):
        here = of(i, rows)
        return here + 0.25 * (of(i + 1, rows) + of(i - 1, rows) + east_of(here) + west_of(here))

    def field(i, rows):
        if 0 <= i < 2:
            return scaled[i, rows, :]
        return s6[i + 2, rows, :].astype(F32)

    for i in range(-1, 3):
        for at, size in CHUNKS:
            rows = pl.ds(at, size)
            za[i + 1, rows, :] = inside(i, smooth(field, i, rows))
    for i in range(2):
        for at, size in CHUNKS:
            rows = pl.ds(at, size)
            zb[i, rows, :] = smooth(lambda j, r: za[j + 1, r, :], i, rows)
    for i in range(2):
        za[i] = product(mats, 6, zb[i])
    for i in range(2):
        zb[i] = product(mats, 4, za[i])
    for i in range(2):
        for at, size in CHUNKS:
            rows = pl.ds(at, size)
            ens[i, rows, :] = (
                0.5 * (spread[i, rows, :] * zb[i, rows, :])
                + (0.5 / (NENS - 1)) * ens[i, rows, :]
                + incr[i, rows, :]
            )

    pass_on([QEN + 1, QEN + 2, QEN + 3])

    @pl.when(has_next)
    def _():
        await_lat([LNX, LNX + 1])

        def transport_back(of, i, rows):
            _, _, east, west, centre = weights(i)
            north, south = weights(i - 1)[0], weights(i + 1)[1]
            here = of(i, rows)
            total = centre * here + north * of(i - 1, rows) + south * of(i + 1, rows)
            return total + west_of(east * here) + east_of(west * here)

        for i in range(6):
            zb[i] = product_16(mats, 2, l6[i])
        for i in range(-1, 3):
            for at, size in CHUNKS:
                rows = pl.ds(at, size)
                za[i + 1, rows, :] = inside(
                    i, transport_back(lambda j, r: zb[j + 2, r, :], i, rows)
                )
        for i in range(4):
            zb[i] = product(mats, 2, za[i])
        for i in range(2):
            for at, size in CHUNKS:
                rows = pl.ds(at, size)
                back = transport_back(lambda j, r: zb[j + 1, r, :], i, rows)
                incr_out[i, rows, :] = lam[i, rows, :] - back

    @pl.when(jnp.logical_not(has_next))
    def _():
        incr_out[...] = lam[...]

    await_lat([QEN + m for m in range(NENS)])

    @pl.when(has_prev)
    def _():
        prop_from = [
            pltpu.make_async_remote_copy(
                prop_send.at[row], arrived.at[row], tm_send.at[2 + row], tm_recv.at[2 + row],
                device_id={"tm": tm - 1}, device_id_type=MESH,
            )
            for row in range(2)
        ]
        for copy in prop_from:
            copy.wait_recv()

    for i in range(2):
        for at, size in CHUNKS:
            rows = pl.ds(at, size)
            near = None
            for m in range(NENS):
                term = members[i, m, rows, :].astype(F32) * q_recv[i, m, rows, :].astype(F32)
                near = term if m == 0 else near + term
            lam_out[i, rows, :] = (
                ens[i, rows, :]
                + (0.5 * 0.25 / (NENS - 1)) * near
                - arrived[i, rows, :].astype(F32)
            )

    @pl.when(has_prev)
    def _():
        dual_to_prev(0).wait_send()
        dual_to_prev(1).wait_send()

    @pl.when(has_next)
    def _():
        prop_to_next(0).wait_send()
        prop_to_next(1).wait_send()

    for up, has in ((True, has_up), (False, has_dn)):

        @pl.when(has)
        def _():
            for item in [SCA, SCA + 1] + [QEN + m for m in range(NENS)]:
                to_lat(item, up).wait_send()

        @pl.when(has & has_next)
        def _():
            for item in [WIN, INC, INC + 1, LNX, LNX + 1]:
                to_lat(item, up).wait_send()

    for up, cond in ((True, fwd_up), (False, fwd_dn)):

        @pl.when(cond)
        def _():
            for item in ROUTED:
                from_fwd(item, up).wait_send()


def per_device(lam, incr, winds, mixing, spread, vert_corr, members):
    row = (COMP, LON)
    vmem = pl.BlockSpec(memory_space=pltpu.VMEM)
    state = jax.ShapeDtypeStruct((2, *row), F32)
    dma = pltpu.SemaphoreType.DMA
    scratch = [
        pltpu.VMEM((6, *row), BF16),
        pltpu.VMEM((6, *row), BF16),
        pltpu.VMEM((6, *row), BF16),
        pltpu.VMEM((3, 8, LON), F32),
        pltpu.VMEM((2, NENS, *row), BF16),
        pltpu.VMEM((2, NENS, *row), BF16),
        pltpu.VMEM((2, *row), BF16),
        pltpu.VMEM((2, *row), BF16),
        pltpu.VMEM((2, *row), BF16),
        pltpu.VMEM((len(ROUTED), *row), BF16),
        pltpu.VMEM((8, COMP, COMP), BF16),
        pltpu.VMEM((2, *row), F32),
        pltpu.VMEM((4, *row), F32),
        pltpu.VMEM((6, *row), F32),
        pltpu.VMEM((2, *row), F32),
        dma((4,)),
        dma((4,)),
        dma((ITEMS,)),
        dma((ITEMS,)),
        dma((ITEMS,)),
        dma((ITEMS,)),
        dma((len(ROUTED),)),
        dma((len(ROUTED),)),
    ]
    lam_result, incr_result = pl.pallas_call(
        kernel,
        out_shape=(state, state),
        in_specs=[vmem] * 7,
        out_specs=(vmem, vmem),
        scratch_shapes=scratch,
        compiler_params=pltpu.CompilerParams(
            collective_id=0, has_side_effects=True, vmem_limit_bytes=48 * 2**20
        ),
    )(
        lam[0],
        incr[0],
        winds[0].reshape(8, LON),
        mixing[0],
        spread[0],
        vert_corr,
        members[0],
    )
    return lam_result[None], incr_result[None]


def solution(mesh):
    in_specs = (
        P("tm", "lat", None, None),
        P("tm", "lat", None, None),
        P("tm", None, "lat", None),
        P("tm", None, None),
        P("tm", "lat", None, None),
        P(),
        P("tm", "lat", None, None, None),
    )
    out_specs = (P("tm", "lat", None, None), P("tm", "lat", None, None))
    return jax.shard_map(
        per_device, mesh=mesh, in_specs=in_specs, out_specs=out_specs, check_vma=False
    )
```

time: 108 us -> 42.2 us (0.39)
  the two profiles are of different devices: /device:TPU:189 before, /device:TPU:390 now
where the time goes in v1:
time: 42.2 us; the launch traced here: 41.8 us
  Pallas kernels  32.8 us (78%)
  local copies, waits for them, and re-layouts  8.3 us (20%)
  between operations  0.66 us (2%)
    pallas_call x1, Pallas kernels, per_device(): pl.pallas_call(kernel, out_shape=(state, state), in_specs=[vmem] * 7, out...  32.8 us
    unnamed x16, local copies, waits for them, and re-layouts  8.29 us

profile of v1, /device:TPU:390, one launch (start us, length us, event | category | flops | bytes accessed | tf_op | source)
XLA Modules:
  0.0 41.8 jit_solution(14594216217869350634)
XLA Ops:
  0.6 0.0 copy-start.6
  0.6 0.7 %copy-done.6 = f32[1,4,2,256]{3,2,1,0:T(2,128)S(1)} copy-done((f32[1,4,2,256]{3,2,1,0:T(2,128)S(1)}, f32[1,4,2,256]{3,2,1,0:T(2,128)}, u32[]{:S(2)}) %copy-start.6) | copy-done | bytes 8216
  1.3 0.0 copy-start
  1.3 1.2 %copy-done = bf16[1,2,4,216,256]{4,3,2,1,0:T(8,128)(2,1)S(1)} copy-done((bf16[1,2,4,216,256]{4,3,2,1,0:T(8,128)(2,1)S(1)}, bf16[1,2,4,216,256]{4,3,2,1,0:T(8,128)(2,1)}, u32[]{:S(2)}) %copy-start) | copy-done | bytes 884760
  2.5 0.0 copy-start.1
  2.5 1.0 %copy-done.1 = f32[1,2,216,256]{3,2,1,0:T(8,128)S(1)} copy-done((f32[1,2,216,256]{3,2,1,0:T(8,128)S(1)}, f32[1,2,216,256]{3,2,1,0:T(8,128)}, u32[]{:S(2)}) %copy-start.1) | copy-done | bytes 442392
  3.5 0.0 copy-start.2
  3.5 1.0 %copy-done.2 = f32[1,2,216,256]{3,2,1,0:T(8,128)S(1)} copy-done((f32[1,2,216,256]{3,2,1,0:T(8,128)S(1)}, f32[1,2,216,256]{3,2,1,0:T(8,128)}, u32[]{:S(2)}) %copy-start.2) | copy-done | bytes 442392
  4.5 0.0 copy-start.3
  4.5 1.0 %copy-done.3 = f32[1,2,216,256]{3,2,1,0:T(8,128)S(1)} copy-done((f32[1,2,216,256]{3,2,1,0:T(8,128)S(1)}, f32[1,2,216,256]{3,2,1,0:T(8,128)}, u32[]{:S(2)}) %copy-start.3) | copy-done | bytes 442392
  5.5 0.0 copy-start.4
  5.5 0.9 %copy-done.4 = f32[1,216,216]{2,1,0:T(8,128)S(1)} copy-done((f32[1,216,216]{2,1,0:T(8,128)S(1)}, f32[1,216,216]{2,1,0:T(8,128)}, u32[]{:S(2)}) %copy-start.4) | copy-done | bytes 186648
  6.5 0.0 copy-start.5
  6.5 0.9 %copy-done.5 = f32[216,216]{1,0:T(8,128)S(1)} copy-done((f32[216,216]{1,0:T(8,128)S(1)}, f32[216,216]{1,0:T(8,128)}, u32[]{:S(2)}) %copy-start.5) | copy-done | bytes 186648
  7.4 32.8 %shard_map.86 = (f32[2,216,256]{2,1,0:T(8,128)S(1)}, f32[2,216,256]{2,1,0:T(8,128)S(1)}) custom-call(f32[2,216,256]{2,1,0:T(8,128)S(1)} %bitcast.10, f32[2,216,256]{2,1,0:T(8,128)S(1)} %bitcast.11, f32[8,256]{1,0:T(8,128)S(1)} %reshape_squeeze.3.winds, f32[216,216]{1,0:T(8,128)S(1)} %bitcast.13, f32[2,216,256]{2,1,0:T(8,128)S(1)} %bitcast.12, ...), custom_call_target="tpu_custom_call" | custom-call | tf_op jit(solution)/shard_map/pallas_call | solution.py:443
  40.3 0.8 %copy.11 = f32[1,2,216,256]{3,2,1,0:T(8,128)} copy(f32[1,2,216,256]{3,2,1,0:T(8,128)S(1)} %bitcast.9) | data formatting | bytes 884736
  41.0 0.8 %copy.12 = f32[1,2,216,256]{3,2,1,0:T(8,128)} copy(f32[1,2,216,256]{3,2,1,0:T(8,128)S(1)} %bitcast.8) | data formatting | bytes 884736
  (1 shorter events, 0.0 us)
Async XLA Ops:
  0.6 0.7 %copy-start.6 = (f32[1,4,2,256]{3,2,1,0:T(2,128)S(1)}, f32[1,4,2,256]{3,2,1,0:T(2,128)}, u32[]{:S(2)}) copy-start(f32[1,4,2,256]{3,2,1,0:T(2,128)} %param.9) | copy-start | bytes 24580
  1.3 1.2 %copy-start = (bf16[1,2,4,216,256]{4,3,2,1,0:T(8,128)(2,1)S(1)}, bf16[1,2,4,216,256]{4,3,2,1,0:T(8,128)(2,1)}, u32[]{:S(2)}) copy-start(bf16[1,2,4,216,256]{4,3,2,1,0:T(8,128)(2,1)} %param.13) | copy-start | bytes 2654212
  2.5 1.0 %copy-start.1 = (f32[1,2,216,256]{3,2,1,0:T(8,128)S(1)}, f32[1,2,216,256]{3,2,1,0:T(8,128)}, u32[]{:S(2)}) copy-start(f32[1,2,216,256]{3,2,1,0:T(8,128)} %param.7) | copy-start | bytes 1327108
  3.5 1.0 %copy-start.2 = (f32[1,2,216,256]{3,2,1,0:T(8,128)S(1)}, f32[1,2,216,256]{3,2,1,0:T(8,128)}, u32[]{:S(2)}) copy-start(f32[1,2,216,256]{3,2,1,0:T(8,128)} %param.8) | copy-start | bytes 1327108
  4.5 1.0 %copy-start.3 = (f32[1,2,216,256]{3,2,1,0:T(8,128)S(1)}, f32[1,2,216,256]{3,2,1,0:T(8,128)}, u32[]{:S(2)}) copy-start(f32[1,2,216,256]{3,2,1,0:T(8,128)} %param.11) | copy-start | bytes 1327108
  5.5 0.9 %copy-start.4 = (f32[1,216,216]{2,1,0:T(8,128)S(1)}, f32[1,216,216]{2,1,0:T(8,128)}, u32[]{:S(2)}) copy-start(f32[1,216,216]{2,1,0:T(8,128)} %param.10) | copy-start | bytes 559876
  6.5 0.9 %copy-start.5 = (f32[216,216]{1,0:T(8,128)S(1)}, f32[216,216]{1,0:T(8,128)}, u32[]{:S(2)}) copy-start(f32[216,216]{1,0:T(8,128)} %vert.1) | copy-start | bytes 559876

commit v2 on v1

--- a/solution.py
+++ b/solution.py
@@ -13,7 +13,13 @@
 
 WIN, INC, SCA, LNX, QEN = 0, 1, 3, 5, 7
 ITEMS = 11
-ROUTED = (SCA, SCA + 1, QEN + 1, QEN + 2, QEN + 3)
+PLACES = {"seven": 14, "six": 12, "one": 2}
+ROUTES = {
+    "seven": (SCA, SCA + 1, LNX + 1),
+    "six": (QEN, QEN + 1),
+    "one": (QEN + 2, QEN + 3),
+}
+ROUTED = {item: (kind, at) for kind, items in ROUTES.items() for at, item in enumerate(items)}
 
 
 def split(value):
@@ -43,10 +49,11 @@
 
 
 def kernel(
-    lam, incr, winds, mixing, spread, vert, members, lam_out, incr_out,
+    lam_hbm, incr_hbm, winds_hbm, mixing_hbm, spread_hbm, vert_hbm, members_hbm, lam_out, incr_out,
+    lam, incr, mixing, spread, vert, members,
     i6, l6, s6, w3, q_send, q_recv, lam_send, prop_send, arrived, fwd,
     mats, scaled, za, zb, ens,
-    tm_send, tm_recv, up_send, up_recv, dn_send, dn_recv, f_in, f_out,
+    load_sem, tm_send, tm_recv, up_send, up_recv, dn_send, dn_recv, f_in, f_out,
 ):
     tm, lat = lax.axis_index("tm"), lax.axis_index("lat")
     place = lax.rem(lat, BAND)
@@ -54,20 +61,43 @@
     has_next, has_prev = tm < TM - 1, tm > 0
     cross_up = (place == BAND - 1) & has_up
     cross_dn = (place == 0) & has_dn
-    fwd_up = (place == BAND - 2) & (lat >= BAND)
-    fwd_dn = (place == 1) & (lat < LAT - BAND)
+
+    def passes(kind, up):
+        if up:
+            return (place == PLACES[kind]) & (lat >= BAND)
+        return (place == BAND - 1 - PLACES[kind]) & (lat < LAT - BAND)
+
+    loads = [
+        pltpu.make_async_copy(src, dst, load_sem.at[at])
+        for at, (src, dst) in enumerate(
+            (
+                (lam_hbm, lam),
+                (spread_hbm, spread),
+                (incr_hbm, incr),
+                (winds_hbm, w3.at[1]),
+                (members_hbm, members),
+                (mixing_hbm, mixing),
+                (vert_hbm, vert),
+            )
+        )
+    ]
+    for load in loads:
+        load.start()
 
     barrier = pltpu.get_barrier_semaphore()
-    greetings = (
+    greetings = [
         (has_next, {"tm": tm + 1}),
         (has_prev, {"tm": tm - 1}),
         (has_up, {"lat": lat + 1}),
         (has_dn, {"lat": lat - 1}),
-        (cross_up, {"lat": lat - (BAND - 2)}),
-        (cross_dn, {"lat": lat + (BAND - 2)}),
-        (fwd_up, {"lat": lat - (BAND - 1)}),
-        (fwd_dn, {"lat": lat + (BAND - 1)}),
-    )
+    ]
+    for kind, p in PLACES.items():
+        greetings += [
+            (cross_up, {"lat": lat - p}),
+            (cross_dn, {"lat": lat + p}),
+            (passes(kind, True), {"lat": lat - p - 1}),
+            (passes(kind, False), {"lat": lat + p + 1}),
+        ]
     targets = 0
     for cond, where in greetings:
         targets = targets + jnp.where(cond, 1, 0)
@@ -96,24 +126,28 @@
 
     def to_fwd(item, up):
         src, _ = ends(item, up)
-        at = ROUTED.index(item)
+        kind, at = ROUTED[item]
         send = up_send if up else dn_send
-        where = {"lat": lat + (BAND - 1) if up else lat - (BAND - 1)}
+        p = PLACES[kind]
+        where = {"lat": lat + p + 1 if up else lat - p - 1}
         return pltpu.make_async_remote_copy(
             src, fwd.at[at], send.at[item], f_in.at[at], device_id=where, device_id_type=MESH
         )
 
     def from_fwd(item, up):
         _, dst = ends(item, up)
-        at = ROUTED.index(item)
+        kind, at = ROUTED[item]
         recv = up_recv if up else dn_recv
-        where = {"lat": lat - (BAND - 2) if up else lat + (BAND - 2)}
+        p = PLACES[kind]
+        where = {"lat": lat - p if up else lat + p}
         return pltpu.make_async_remote_copy(
             fwd.at[at], dst, f_out.at[at], recv.at[item], device_id=where, device_id_type=MESH
         )
 
-    def start_lat(items, cond=True):
+    def start_lat(items, cond=True, crossing=None):
         for up, has, cross in ((True, has_up, cross_up), (False, has_dn, cross_dn)):
+            if crossing is not None:
+                has = has & (cross if crossing else jnp.logical_not(cross))
             plain = [item for item in items if item not in ROUTED]
             routed = [item for item in items if item in ROUTED]
 
@@ -129,27 +163,27 @@
                     for item in routed:
                         to_lat(item, up).start()
 
-                @pl.when(cross & cond)
+                @pl.when(has & cross & cond)
                 def _():
                     for item in routed:
                         to_fwd(item, up).start()
 
-    def pass_on(items):
-        for up, cond in ((True, fwd_up), (False, fwd_dn)):
-
-            @pl.when(cond)
-            def _():
-                for item in items:
-                    copy = from_fwd(item, up)
-                    pltpu.make_async_remote_copy(
-                        fwd.at[ROUTED.index(item)],
-                        fwd.at[ROUTED.index(item)],
-                        f_out.at[ROUTED.index(item)],
-                        f_in.at[ROUTED.index(item)],
-                        device_id={"lat": lat - 1 if up else lat + 1},
-                        device_id_type=MESH,
-                    ).wait_recv()
-                    copy.start()
+    def pass_on(items, cond=True):
+        for kind, routed in ROUTES.items():
+            now = [item for item in items if item in routed]
+            if not now:
+                continue
+            for up in (True, False):
+
+                @pl.when(passes(kind, up) & cond)
+                def _():
+                    for item in now:
+                        at = ROUTED[item][1]
+                        pltpu.make_async_remote_copy(
+                            fwd.at[at], fwd.at[at], f_out.at[at], f_in.at[at],
+                            device_id={"lat": lat - 1 if up else lat + 1}, device_id_type=MESH,
+                        ).wait_recv()
+                        from_fwd(item, up).start()
 
     def await_lat(items, cond=True):
         for up, has in ((True, has_dn), (False, has_up)):
@@ -171,7 +205,8 @@
             device_id={"tm": tm + 1}, device_id_type=MESH,
         )
 
-    w3[1] = winds[...]
+    for load in loads[:4]:
+        load.wait()
     for row in range(2):
         for at, size in CHUNKS:
             rows = pl.ds(at, size)
@@ -214,6 +249,8 @@
     start_lat([WIN, INC, INC + 1], has_next)
     start_lat([SCA, SCA + 1])
 
+    for load in loads[4:]:
+        load.wait()
     for base, matrix in ((0, mixing[...]), (4, vert[...])):
         mats[base], mats[base + 1] = split(matrix)
         mats[base + 2], mats[base + 3] = split(matrix.T)
@@ -233,9 +270,12 @@
         for row in range(2):
             ens[row, rows, :] = totals[row]
 
+    edges = [QEN + m for m in range(NENS)]
+    start_lat(edges, crossing=True)
+
     def weights(i):
         block, row = (i + 2) // 2, (i + 2) % 2
-        north, south, east, west = (w3[block, 2 * p + row : 2 * p + row + 1, :] for p in range(4))
+        north, south, east, west = (w3[block, p, row : row + 1, :] for p in range(4))
         return north, south, east, west, 1.0 - north - south - east - west
 
     low_edge = jnp.where(has_dn, 1.0, 0.0).astype(F32)
@@ -277,6 +317,8 @@
             prop_send[i] = product(mats, 0, za[i]).astype(BF16)
             prop_to_next(i).start()
 
+    pass_on([SCA, SCA + 1])
+
     for row in range(2):
 
         @pl.when(has_next)
@@ -285,9 +327,10 @@
 
         start_lat([LNX + row], has_next)
 
-    start_lat([QEN + m for m in range(NENS)])
-
-    pass_on([SCA, SCA + 1])
+    start_lat(edges, crossing=False)
+
+    pass_on(edges)
+    pass_on([LNX + 1], has_next)
     await_lat([SCA, SCA + 1])
 
     def smooth(of, i, rows):
@@ -320,8 +363,6 @@
                 + incr[i, rows, :]
             )
 
-    pass_on([QEN + 1, QEN + 2, QEN + 3])
-
     @pl.when(has_next)
     def _():
         await_lat([LNX, LNX + 1])
@@ -353,7 +394,7 @@
     def _():
         incr_out[...] = lam[...]
 
-    await_lat([QEN + m for m in range(NENS)])
+    await_lat(edges)
 
     @pl.when(has_prev)
     def _():
@@ -394,7 +435,7 @@
 
         @pl.when(has)
         def _():
-            for item in [SCA, SCA + 1] + [QEN + m for m in range(NENS)]:
+            for item in [SCA, SCA + 1, *edges]:
                 to_lat(item, up).wait_send()
 
         @pl.when(has & has_next)
@@ -402,12 +443,13 @@
             for item in [WIN, INC, INC + 1, LNX, LNX + 1]:
                 to_lat(item, up).wait_send()
 
-    for up, cond in ((True, fwd_up), (False, fwd_dn)):
-
-        @pl.when(cond)
-        def _():
-            for item in ROUTED:
-                from_fwd(item, up).wait_send()
+    for kind, routed in ROUTES.items():
+        for up in (True, False):
+            for item in routed:
+
+                @pl.when(passes(kind, up) & (has_next if item in (LNX, LNX + 1) else True))
+                def _():
+                    from_fwd(item, up).wait_send()
 
 
 def per_device(lam, incr, winds, mixing, spread, vert_corr, members):
@@ -416,43 +458,50 @@
     state = jax.ShapeDtypeStruct((2, *row), F32)
     dma = pltpu.SemaphoreType.DMA
     scratch = [
+        pltpu.VMEM((2, *row), F32),
+        pltpu.VMEM((2, *row), F32),
+        pltpu.VMEM((COMP, COMP), F32),
+        pltpu.VMEM((2, *row), F32),
+        pltpu.VMEM((COMP, COMP), F32),
+        pltpu.VMEM((2, NENS, *row), BF16),
         pltpu.VMEM((6, *row), BF16),
         pltpu.VMEM((6, *row), BF16),
         pltpu.VMEM((6, *row), BF16),
-        pltpu.VMEM((3, 8, LON), F32),
+        pltpu.VMEM((3, 4, 2, LON), F32),
         pltpu.VMEM((2, NENS, *row), BF16),
         pltpu.VMEM((2, NENS, *row), BF16),
         pltpu.VMEM((2, *row), BF16),
         pltpu.VMEM((2, *row), BF16),
         pltpu.VMEM((2, *row), BF16),
-        pltpu.VMEM((len(ROUTED), *row), BF16),
+        pltpu.VMEM((3, *row), BF16),
         pltpu.VMEM((8, COMP, COMP), BF16),
         pltpu.VMEM((2, *row), F32),
         pltpu.VMEM((4, *row), F32),
         pltpu.VMEM((6, *row), F32),
         pltpu.VMEM((2, *row), F32),
+        dma((7,)),
         dma((4,)),
         dma((4,)),
         dma((ITEMS,)),
         dma((ITEMS,)),
         dma((ITEMS,)),
         dma((ITEMS,)),
-        dma((len(ROUTED),)),
-        dma((len(ROUTED),)),
+        dma((3,)),
+        dma((3,)),
     ]
     lam_result, incr_result = pl.pallas_call(
         kernel,
         out_shape=(state, state),
-        in_specs=[vmem] * 7,
+        in_specs=[pl.BlockSpec(memory_space=pltpu.HBM)] * 7,
         out_specs=(vmem, vmem),
         scratch_shapes=scratch,
         compiler_params=pltpu.CompilerParams(
-            collective_id=0, has_side_effects=True, vmem_limit_bytes=48 * 2**20
+            collective_id=0, has_side_effects=True, vmem_limit_bytes=60 * 2**20
         ),
     )(
         lam[0],
         incr[0],
-        winds[0].reshape(8, LON),
+        winds[0],
         mixing[0],
         spread[0],
         vert_corr,

time: 42.2 us -> 34.7 us (0.82)
  the two profiles are of different devices: /device:TPU:390 before, /device:TPU:200 now
where the time goes in v2:
time: 34.7 us; the launch traced here: 34.5 us
  Pallas kernels  31.2 us (90%)
  local copies, waits for them, and re-layouts  2.62 us (8%)
  between operations  0.65 us (2%)
    pallas_call x1, Pallas kernels, per_device(): pl.pallas_call(kernel, out_shape=(state, state), in_specs=[pl.BlockSpec(m...  31.2 us
    unnamed x4, local copies, waits for them, and re-layouts  2.62 us

profile of v2, /device:TPU:200, one launch (start us, length us, event | category | flops | bytes accessed | tf_op | source)
XLA Modules:
  0.0 34.5 jit_solution(1575309126024807877)
XLA Ops:
  0.6 31.2 %shard_map.86 = (f32[2,216,256]{2,1,0:T(8,128)}, f32[2,216,256]{2,1,0:T(8,128)}) custom-call(f32[2,216,256]{2,1,0:T(8,128)} %bitcast.11, f32[2,216,256]{2,1,0:T(8,128)} %bitcast.12, f32[4,2,256]{2,1,0:T(2,128)} %bitcast.15, f32[216,216]{1,0:T(8,128)} %bitcast.14, f32[2,216,256]{2,1,0:T(8,128)} %bitcast.13, f32[216,216]{1,0:T(8,128)} %vert_hbm.1, ...), custom_call_target="tpu_custom_call" | custom-call | tf_op jit(solution)/shard_map/pallas_call | solution.py:492
  31.8 0.0 copy-start
  31.9 1.9 %copy.11 = f32[1,2,216,256]{3,2,1,0:T(8,128)} copy(f32[1,2,216,256]{3,2,1,0:T(8,128)} %bitcast.10) | data formatting | bytes 884736
  33.7 0.0 copy-done
  33.7 0.8 %copy.12 = f32[1,2,216,256]{3,2,1,0:T(8,128)} copy(f32[1,2,216,256]{3,2,1,0:T(8,128)S(1)} %bitcast.9) | data formatting | bytes 884736
Async XLA Ops:
  31.8 1.9 %copy-start = (f32[2,216,256]{2,1,0:T(8,128)S(1)}, f32[2,216,256]{2,1,0:T(8,128)}, u32[]{:S(2)}) copy-start(f32[2,216,256]{2,1,0:T(8,128)} %get-tuple-element.5) | copy-start | bytes 1327108

commit v3 on v2

--- a/solution.py
+++ b/solution.py
@@ -15,11 +15,20 @@
 ITEMS = 11
 PLACES = {"seven": 14, "six": 12, "one": 2}
 ROUTES = {
-    "seven": (SCA, SCA + 1, LNX + 1),
-    "six": (QEN, QEN + 1),
-    "one": (QEN + 2, QEN + 3),
+    "seven": (INC, INC + 1, QEN, QEN + 1),
+    "six": (SCA, SCA + 1, QEN + 2, QEN + 3),
+    "one": (SCA, SCA + 1, QEN + 2, QEN + 3),
 }
-ROUTED = {item: (kind, at) for kind, items in ROUTES.items() for at, item in enumerate(items)}
+KINDS = {True: ("seven", "six"), False: ("one",)}
+FAR = len(ROUTES["seven"])
+SLOTS = FAR + 2
+
+
+def route(item, even):
+    for kind in KINDS[even]:
+        if item in ROUTES[kind]:
+            return kind, ROUTES[kind].index(item)
+    return None
 
 
 def split(value):
@@ -53,7 +62,7 @@
     lam, incr, mixing, spread, vert, members,
     i6, l6, s6, w3, q_send, q_recv, lam_send, prop_send, arrived, fwd,
     mats, scaled, za, zb, ens,
-    load_sem, tm_send, tm_recv, up_send, up_recv, dn_send, dn_recv, f_in, f_out,
+    load_sem, tm_send, tm_recv, up_send, up_recv, dn_send, dn_recv, f_in, f_out, far_send,
 ):
     tm, lat = lax.axis_index("tm"), lax.axis_index("lat")
     place = lax.rem(lat, BAND)
@@ -62,10 +71,28 @@
     cross_up = (place == BAND - 1) & has_up
     cross_dn = (place == 0) & has_dn
 
-    def passes(kind, up):
+    is_even = lax.rem(tm, 2) == 0
+    is_odd = jnp.logical_not(is_even)
+
+    def at_place(kind, up):
         if up:
             return (place == PLACES[kind]) & (lat >= BAND)
         return (place == BAND - 1 - PLACES[kind]) & (lat < LAT - BAND)
+
+    def of_tm(kind):
+        return is_even if kind in KINDS[True] else is_odd
+
+    def passes(kind, up):
+        return at_place(kind, up) & of_tm(kind)
+
+    def straight(up):
+        return is_even if up else is_odd
+
+    def passes_dual(up):
+        return at_place("seven", up) & straight(up) & has_next
+
+    def sends_dual(up):
+        return (cross_up if up else cross_dn) & jnp.logical_not(straight(up)) & has_prev
 
     loads = [
         pltpu.make_async_copy(src, dst, load_sem.at[at])
@@ -86,21 +113,25 @@
 
     barrier = pltpu.get_barrier_semaphore()
     greetings = [
-        (has_next, {"tm": tm + 1}),
-        (has_prev, {"tm": tm - 1}),
-        (has_up, {"lat": lat + 1}),
-        (has_dn, {"lat": lat - 1}),
+        (has_next, {"tm": tm + 1}, has_prev),
+        (has_prev, {"tm": tm - 1}, has_next),
+        (has_up, {"lat": lat + 1}, has_dn),
+        (has_dn, {"lat": lat - 1}, has_up),
+        (cross_up & is_odd & has_next, {"lat": lat - PLACES["seven"]}, passes_dual(False)),
+        (passes_dual(True), {"tm": tm + 1, "lat": lat - PLACES["seven"] - 1}, sends_dual(True)),
+        (passes_dual(False), {"tm": tm + 1, "lat": lat + PLACES["seven"] + 1}, sends_dual(False)),
+        (cross_up & is_even & has_next, {"tm": tm + 1, "lat": lat + 1}, cross_dn & is_odd & has_prev),
     ]
     for kind, p in PLACES.items():
         greetings += [
-            (cross_up, {"lat": lat - p}),
-            (cross_dn, {"lat": lat + p}),
-            (passes(kind, True), {"lat": lat - p - 1}),
-            (passes(kind, False), {"lat": lat + p + 1}),
+            (cross_up & of_tm(kind), {"lat": lat - p}, passes(kind, False)),
+            (cross_dn & of_tm(kind), {"lat": lat + p}, passes(kind, True)),
+            (passes(kind, True), {"lat": lat - p - 1}, cross_up & of_tm(kind)),
+            (passes(kind, False), {"lat": lat + p + 1}, cross_dn & of_tm(kind)),
         ]
     targets = 0
-    for cond, where in greetings:
-        targets = targets + jnp.where(cond, 1, 0)
+    for cond, where, mirrored in greetings:
+        targets = targets + jnp.where(mirrored, 1, 0)
 
         @pl.when(cond)
         def _():
@@ -124,9 +155,22 @@
             src, dst, send.at[item], recv.at[item], device_id=where, device_id_type=MESH
         )
 
-    def to_fwd(item, up):
+    def dual_across(row, up):
+        where = {"tm": tm - 1, "lat": lat + BAND - 1 if up else lat - BAND + 1}
+        return pltpu.make_async_remote_copy(
+            lam_send.at[row], fwd.at[FAR + row], far_send.at[row], f_in.at[FAR + row],
+            device_id=where, device_id_type=MESH,
+        )
+
+    def dual_direct(row):
+        return pltpu.make_async_remote_copy(
+            lam_send.at[row], l6.at[4 + row], far_send.at[row], dn_recv.at[LNX + row],
+            device_id={"tm": tm - 1, "lat": lat - 1}, device_id_type=MESH,
+        )
+
+    def to_fwd(item, up, even):
         src, _ = ends(item, up)
-        kind, at = ROUTED[item]
+        kind, at = route(item, even)
         send = up_send if up else dn_send
         p = PLACES[kind]
         where = {"lat": lat + p + 1 if up else lat - p - 1}
@@ -134,9 +178,8 @@
             src, fwd.at[at], send.at[item], f_in.at[at], device_id=where, device_id_type=MESH
         )
 
-    def from_fwd(item, up):
+    def from_fwd(item, kind, at, up):
         _, dst = ends(item, up)
-        kind, at = ROUTED[item]
         recv = up_recv if up else dn_recv
         p = PLACES[kind]
         where = {"lat": lat - p if up else lat + p}
@@ -144,29 +187,33 @@
             fwd.at[at], dst, f_out.at[at], recv.at[item], device_id=where, device_id_type=MESH
         )
 
-    def start_lat(items, cond=True, crossing=None):
+    def start_lat(items, cond=True, sides=(True, False)):
         for up, has, cross in ((True, has_up, cross_up), (False, has_dn, cross_dn)):
-            if crossing is not None:
-                has = has & (cross if crossing else jnp.logical_not(cross))
-            plain = [item for item in items if item not in ROUTED]
-            routed = [item for item in items if item in ROUTED]
-
-            @pl.when(has & cond)
-            def _():
-                for item in plain:
-                    to_lat(item, up).start()
-
-            if routed:
+            if False in sides:
 
                 @pl.when(has & jnp.logical_not(cross) & cond)
                 def _():
-                    for item in routed:
+                    for item in items:
                         to_lat(item, up).start()
 
-                @pl.when(has & cross & cond)
+            if True not in sides:
+                continue
+            for even in (True, False):
+
+                @pl.when(cross & (is_even if even else is_odd) & cond)
                 def _():
-                    for item in routed:
-                        to_fwd(item, up).start()
+                    for item in items:
+                        if route(item, even):
+                            to_fwd(item, up, even).start()
+                        elif item not in (LNX, LNX + 1) or (up and not even):
+                            to_lat(item, up).start()
+
+    def hand_over(item, kind, at, up):
+        pltpu.make_async_remote_copy(
+            fwd.at[at], fwd.at[at], f_out.at[at], f_in.at[at],
+            device_id={"lat": lat - 1 if up else lat + 1}, device_id_type=MESH,
+        ).wait_recv()
+        from_fwd(item, kind, at, up).start()
 
     def pass_on(items, cond=True):
         for kind, routed in ROUTES.items():
@@ -178,12 +225,15 @@
                 @pl.when(passes(kind, up) & cond)
                 def _():
                     for item in now:
-                        at = ROUTED[item][1]
-                        pltpu.make_async_remote_copy(
-                            fwd.at[at], fwd.at[at], f_out.at[at], f_in.at[at],
-                            device_id={"lat": lat - 1 if up else lat + 1}, device_id_type=MESH,
-                        ).wait_recv()
-                        from_fwd(item, up).start()
+                        hand_over(item, kind, routed.index(item), up)
+
+    def pass_duals():
+        for up in (True, False):
+
+            @pl.when(passes_dual(up))
+            def _():
+                for row in range(2):
+                    hand_over(LNX + row, "seven", FAR + row, up)
 
     def await_lat(items, cond=True):
         for up, has in ((True, has_dn), (False, has_up)):
@@ -248,6 +298,17 @@
 
     start_lat([WIN, INC, INC + 1], has_next)
     start_lat([SCA, SCA + 1])
+    for up in (True, False):
+
+        @pl.when(sends_dual(up))
+        def _():
+            for row in range(2):
+                dual_across(row, up).start()
+
+    @pl.when(cross_dn & is_odd & has_prev)
+    def _():
+        for row in range(2):
+            dual_direct(row).start()
 
     for load in loads[4:]:
         load.wait()
@@ -271,7 +332,8 @@
             ens[row, rows, :] = totals[row]
 
     edges = [QEN + m for m in range(NENS)]
-    start_lat(edges, crossing=True)
+    start_lat(edges, sides=(True,))
+    pass_on([INC, INC + 1], has_next)
 
     def weights(i):
         block, row = (i + 2) // 2, (i + 2) % 2
@@ -318,6 +380,7 @@
             prop_to_next(i).start()
 
     pass_on([SCA, SCA + 1])
+    pass_duals()
 
     for row in range(2):
 
@@ -327,10 +390,9 @@
 
         start_lat([LNX + row], has_next)
 
-    start_lat(edges, crossing=False)
-
+    start_lat(edges, sides=(False,))
     pass_on(edges)
-    pass_on([LNX + 1], has_next)
+
     await_lat([SCA, SCA + 1])
 
     def smooth(of, i, rows):
@@ -431,7 +493,12 @@
         prop_to_next(0).wait_send()
         prop_to_next(1).wait_send()
 
-    for up, has in ((True, has_up), (False, has_dn)):
+    @pl.when(cross_dn & is_odd & has_prev)
+    def _():
+        for row in range(2):
+            dual_direct(row).wait_send()
+
+    for up, has, cross in ((True, has_up, cross_up), (False, has_dn, cross_dn)):
 
         @pl.when(has)
         def _():
@@ -440,16 +507,30 @@
 
         @pl.when(has & has_next)
         def _():
-            for item in [WIN, INC, INC + 1, LNX, LNX + 1]:
+            for item in [WIN, INC, INC + 1]:
                 to_lat(item, up).wait_send()
 
-    for kind, routed in ROUTES.items():
-        for up in (True, False):
-            for item in routed:
-
-                @pl.when(passes(kind, up) & (has_next if item in (LNX, LNX + 1) else True))
+        @pl.when(has & has_next & (jnp.logical_not(cross) | (is_odd if up else False)))
+        def _():
+            for item in [LNX, LNX + 1]:
+                to_lat(item, up).wait_send()
+
+        @pl.when(sends_dual(up))
+        def _():
+            for row in range(2):
+                dual_across(row, up).wait_send()
+
+        for kind, routed in ROUTES.items():
+            for at, item in enumerate(routed):
+
+                @pl.when(passes(kind, up) & (has_next if item in (INC, INC + 1) else True))
                 def _():
-                    from_fwd(item, up).wait_send()
+                    from_fwd(item, kind, at, up).wait_send()
+
+        @pl.when(passes_dual(up))
+        def _():
+            for row in range(2):
+                from_fwd(LNX + row, "seven", FAR + row, up).wait_send()
 
 
 def per_device(lam, incr, winds, mixing, spread, vert_corr, members):
@@ -473,7 +554,7 @@
         pltpu.VMEM((2, *row), BF16),
         pltpu.VMEM((2, *row), BF16),
         pltpu.VMEM((2, *row), BF16),
-        pltpu.VMEM((3, *row), BF16),
+        pltpu.VMEM((SLOTS, *row), BF16),
         pltpu.VMEM((8, COMP, COMP), BF16),
         pltpu.VMEM((2, *row), F32),
         pltpu.VMEM((4, *row), F32),
@@ -486,8 +567,9 @@
         dma((ITEMS,)),
         dma((ITEMS,)),
         dma((ITEMS,)),
-        dma((3,)),
-        dma((3,)),
+        dma((SLOTS,)),
+        dma((SLOTS,)),
+        dma((2,)),
     ]
     lam_result, incr_result = pl.pallas_call(
         kernel,
@@ -496,16 +578,13 @@
         out_specs=(vmem, vmem),
         scratch_shapes=scratch,
         compiler_params=pltpu.CompilerParams(
-            collective_id=0, has_side_effects=True, vmem_limit_bytes=60 * 2**20
+            collective_id=0, has_side_effects=True, vmem_limit_bytes=48 * 2**20
         ),
     )(
-        lam[0],
-        incr[0],
-        winds[0],
-        mixing[0],
-        spread[0],
-        vert_corr,
-        members[0],
+        *(
+            pltpu.with_memory_space_constraint(array, pltpu.HBM)
+            for array in (lam[0], incr[0], winds[0], mixing[0], spread[0], vert_corr, members[0])
+        )
     )
     return lam_result[None], incr_result[None]
 

time: 34.7 us -> 31 us (0.89)
  the two profiles are of different devices: /device:TPU:200 before, /device:TPU:181 now
where the time goes in v3:
time: 31 us; the launch traced here: 30.9 us
  Pallas kernels  28.7 us (93%)
  local copies, waits for them, and re-layouts  1.53 us (5%)
  between operations  0.64 us (2%)
    pallas_call x1, Pallas kernels, per_device(): pl.pallas_call(kernel, out_shape=(state, state), in_specs=[pl.BlockSpec(m...  28.7 us
    unnamed x2, local copies, waits for them, and re-layouts  1.53 us

profile of v3, /device:TPU:181, one launch (start us, length us, event | category | flops | bytes accessed | tf_op | source)
XLA Modules:
  0.0 30.9 jit_solution(434096363109266462)
XLA Ops:
  0.6 28.7 %shard_map.86 = (f32[2,216,256]{2,1,0:T(8,128)S(1)}, f32[2,216,256]{2,1,0:T(8,128)S(1)}) custom-call(f32[2,216,256]{2,1,0:T(8,128)} %bitcast.11, f32[2,216,256]{2,1,0:T(8,128)} %bitcast.12, f32[4,2,256]{2,1,0:T(2,128)} %bitcast.15, f32[216,216]{1,0:T(8,128)} %bitcast.14, f32[2,216,256]{2,1,0:T(8,128)} %bitcast.13, f32[216,216]{1,0:T(8,128)} %vert_hbm.1, ...), custom_call_target="tpu_custom_call" | custom-call | tf_op jit(solution)/shard_map/pallas_call | solution.py:574
  29.4 0.8 %copy.11 = f32[1,2,216,256]{3,2,1,0:T(8,128)} copy(f32[1,2,216,256]{3,2,1,0:T(8,128)S(1)} %bitcast.9) | data formatting | bytes 884736
  30.1 0.8 %copy.12 = f32[1,2,216,256]{3,2,1,0:T(8,128)} copy(f32[1,2,216,256]{3,2,1,0:T(8,128)S(1)} %bitcast.8) | data formatting | bytes 884736

commit v4 on v3

--- a/solution.py
+++ b/solution.py
@@ -15,19 +15,18 @@
 ITEMS = 11
 PLACES = {"seven": 14, "six": 12, "one": 2}
 ROUTES = {
-    "seven": (INC, INC + 1, QEN, QEN + 1),
-    "six": (SCA, SCA + 1, QEN + 2, QEN + 3),
-    "one": (SCA, SCA + 1, QEN + 2, QEN + 3),
+    True: {"seven": (SCA, SCA + 1, QEN), "six": (QEN + 2, QEN + 3)},
+    False: {"seven": (QEN, QEN + 1), "one": (SCA, SCA + 1, QEN + 2, QEN + 3)},
 }
-KINDS = {True: ("seven", "six"), False: ("one",)}
-FAR = len(ROUTES["seven"])
+RELAYS = [(kind, even) for even, kinds in ROUTES.items() for kind in kinds]
+FAR = 4
 SLOTS = FAR + 2
 
 
 def route(item, even):
-    for kind in KINDS[even]:
-        if item in ROUTES[kind]:
-            return kind, ROUTES[kind].index(item)
+    for kind, items in ROUTES[even].items():
+        if item in items:
+            return kind, items.index(item)
     return None
 
 
@@ -79,11 +78,11 @@
             return (place == PLACES[kind]) & (lat >= BAND)
         return (place == BAND - 1 - PLACES[kind]) & (lat < LAT - BAND)
 
-    def of_tm(kind):
-        return is_even if kind in KINDS[True] else is_odd
-
-    def passes(kind, up):
-        return at_place(kind, up) & of_tm(kind)
+    def of_tm(even):
+        return is_even if even else is_odd
+
+    def passes(kind, even, up):
+        return at_place(kind, up) & of_tm(even)
 
     def straight(up):
         return is_even if up else is_odd
@@ -117,17 +116,16 @@
         (has_prev, {"tm": tm - 1}, has_next),
         (has_up, {"lat": lat + 1}, has_dn),
         (has_dn, {"lat": lat - 1}, has_up),
-        (cross_up & is_odd & has_next, {"lat": lat - PLACES["seven"]}, passes_dual(False)),
         (passes_dual(True), {"tm": tm + 1, "lat": lat - PLACES["seven"] - 1}, sends_dual(True)),
         (passes_dual(False), {"tm": tm + 1, "lat": lat + PLACES["seven"] + 1}, sends_dual(False)),
-        (cross_up & is_even & has_next, {"tm": tm + 1, "lat": lat + 1}, cross_dn & is_odd & has_prev),
     ]
-    for kind, p in PLACES.items():
+    for kind, even in RELAYS:
+        p = PLACES[kind]
         greetings += [
-            (cross_up & of_tm(kind), {"lat": lat - p}, passes(kind, False)),
-            (cross_dn & of_tm(kind), {"lat": lat + p}, passes(kind, True)),
-            (passes(kind, True), {"lat": lat - p - 1}, cross_up & of_tm(kind)),
-            (passes(kind, False), {"lat": lat + p + 1}, cross_dn & of_tm(kind)),
+            (cross_up & of_tm(even), {"lat": lat - p}, passes(kind, even, False)),
+            (cross_dn & of_tm(even), {"lat": lat + p}, passes(kind, even, True)),
+            (passes(kind, even, True), {"lat": lat - p - 1}, cross_up & of_tm(even)),
+            (passes(kind, even, False), {"lat": lat + p + 1}, cross_dn & of_tm(even)),
         ]
     targets = 0
     for cond, where, mirrored in greetings:
@@ -162,12 +160,6 @@
             device_id=where, device_id_type=MESH,
         )
 
-    def dual_direct(row):
-        return pltpu.make_async_remote_copy(
-            lam_send.at[row], l6.at[4 + row], far_send.at[row], dn_recv.at[LNX + row],
-            device_id={"tm": tm - 1, "lat": lat - 1}, device_id_type=MESH,
-        )
-
     def to_fwd(item, up, even):
         src, _ = ends(item, up)
         kind, at = route(item, even)
@@ -205,7 +197,7 @@
                     for item in items:
                         if route(item, even):
                             to_fwd(item, up, even).start()
-                        elif item not in (LNX, LNX + 1) or (up and not even):
+                        elif item not in (LNX, LNX + 1) or even != up:
                             to_lat(item, up).start()
 
     def hand_over(item, kind, at, up):
@@ -215,17 +207,19 @@
         ).wait_recv()
         from_fwd(item, kind, at, up).start()
 
-    def pass_on(items, cond=True):
-        for kind, routed in ROUTES.items():
-            now = [item for item in items if item in routed]
+    def pass_on(items, kinds=tuple(PLACES)):
+        for kind, even in RELAYS:
+            if kind not in kinds:
+                continue
+            now = [item for item in items if item in ROUTES[even][kind]]
             if not now:
                 continue
             for up in (True, False):
 
-                @pl.when(passes(kind, up) & cond)
+                @pl.when(passes(kind, even, up))
                 def _():
                     for item in now:
-                        hand_over(item, kind, routed.index(item), up)
+                        hand_over(item, kind, route(item, even)[1], up)
 
     def pass_duals():
         for up in (True, False):
@@ -304,11 +298,6 @@
         def _():
             for row in range(2):
                 dual_across(row, up).start()
-
-    @pl.when(cross_dn & is_odd & has_prev)
-    def _():
-        for row in range(2):
-            dual_direct(row).start()
 
     for load in loads[4:]:
         load.wait()
@@ -333,7 +322,20 @@
 
     edges = [QEN + m for m in range(NENS)]
     start_lat(edges, sides=(True,))
-    pass_on([INC, INC + 1], has_next)
+    start_lat(edges[:2], sides=(False,))
+    def dual_row(row):
+        @pl.when(has_next)
+        def _():
+            dual_to_prev(row).wait_recv()
+
+        start_lat([LNX + row], has_next)
+
+    pass_on([SCA, SCA + 1])
+    pass_duals()
+    dual_row(0)
+    pass_on(edges, ("six",))
+    dual_row(1)
+    start_lat(edges[2:], sides=(False,))
 
     def weights(i):
         block, row = (i + 2) // 2, (i + 2) % 2
@@ -379,19 +381,7 @@
             prop_send[i] = product(mats, 0, za[i]).astype(BF16)
             prop_to_next(i).start()
 
-    pass_on([SCA, SCA + 1])
-    pass_duals()
-
-    for row in range(2):
-
-        @pl.when(has_next)
-        def _():
-            dual_to_prev(row).wait_recv()
-
-        start_lat([LNX + row], has_next)
-
-    start_lat(edges, sides=(False,))
-    pass_on(edges)
+    pass_on(edges, ("seven", "one"))
 
     await_lat([SCA, SCA + 1])
 
@@ -493,11 +483,6 @@
         prop_to_next(0).wait_send()
         prop_to_next(1).wait_send()
 
-    @pl.when(cross_dn & is_odd & has_prev)
-    def _():
-        for row in range(2):
-            dual_direct(row).wait_send()
-
     for up, has, cross in ((True, has_up, cross_up), (False, has_dn, cross_dn)):
 
         @pl.when(has)
@@ -510,7 +495,7 @@
             for item in [WIN, INC, INC + 1]:
                 to_lat(item, up).wait_send()
 
-        @pl.when(has & has_next & (jnp.logical_not(cross) | (is_odd if up else False)))
+        @pl.when(has & has_next & (jnp.logical_not(cross) | jnp.logical_not(straight(up))))
         def _():
             for item in [LNX, LNX + 1]:
                 to_lat(item, up).wait_send()
@@ -520,11 +505,11 @@
             for row in range(2):
                 dual_across(row, up).wait_send()
 
-        for kind, routed in ROUTES.items():
-            for at, item in enumerate(routed):
-
-                @pl.when(passes(kind, up) & (has_next if item in (INC, INC + 1) else True))
-                def _():
+        for kind, even in RELAYS:
+
+            @pl.when(passes(kind, even, up))
+            def _():
+                for at, item in enumerate(ROUTES[even][kind]):
                     from_fwd(item, kind, at, up).wait_send()
 
         @pl.when(passes_dual(up))

time: 31 us -> 29.4 us (0.948)
  the two profiles are of different devices: /device:TPU:181 before, /device:TPU:390 now
where the time goes in v4:
time: 29.4 us; the launch traced here: 29.2 us
  Pallas kernels  27.1 us (92%)
  local copies, waits for them, and re-layouts  1.53 us (5%)
  between operations  0.64 us (2%)
    pallas_call x1, Pallas kernels, per_device(): pl.pallas_call(kernel, out_shape=(state, state), in_specs=[pl.BlockSpec(m...  27.1 us
    unnamed x2, local copies, waits for them, and re-layouts  1.53 us

profile of v4, /device:TPU:390, one launch (start us, length us, event | category | flops | bytes accessed | tf_op | source)
XLA Modules:
  0.0 29.2 jit_solution(952763557654071701)
XLA Ops:
  0.6 27.1 %shard_map.86 = (f32[2,216,256]{2,1,0:T(8,128)S(1)}, f32[2,216,256]{2,1,0:T(8,128)S(1)}) custom-call(f32[2,216,256]{2,1,0:T(8,128)} %bitcast.11, f32[2,216,256]{2,1,0:T(8,128)} %bitcast.12, f32[4,2,256]{2,1,0:T(2,128)} %bitcast.15, f32[216,216]{1,0:T(8,128)} %bitcast.14, f32[2,216,256]{2,1,0:T(8,128)} %bitcast.13, f32[216,216]{1,0:T(8,128)} %vert_hbm.1, ...), custom_call_target="tpu_custom_call" | custom-call | tf_op jit(solution)/shard_map/pallas_call | solution.py:559
  27.7 0.8 %copy.11 = f32[1,2,216,256]{3,2,1,0:T(8,128)} copy(f32[1,2,216,256]{3,2,1,0:T(8,128)S(1)} %bitcast.9) | data formatting | bytes 884736
  28.5 0.8 %copy.12 = f32[1,2,216,256]{3,2,1,0:T(8,128)} copy(f32[1,2,216,256]{3,2,1,0:T(8,128)S(1)} %bitcast.8) | data formatting | bytes 884736

commit v5 on v4

--- a/solution.py
+++ b/solution.py
@@ -60,7 +60,7 @@
     lam_hbm, incr_hbm, winds_hbm, mixing_hbm, spread_hbm, vert_hbm, members_hbm, lam_out, incr_out,
     lam, incr, mixing, spread, vert, members,
     i6, l6, s6, w3, q_send, q_recv, lam_send, prop_send, arrived, fwd,
-    mats, scaled, za, zb, ens,
+    mats, scaled, ya, za, zb, ens,
     load_sem, tm_send, tm_recv, up_send, up_recv, dn_send, dn_recv, f_in, f_out, far_send,
 ):
     tm, lat = lax.axis_index("tm"), lax.axis_index("lat")
@@ -90,25 +90,10 @@
     def passes_dual(up):
         return at_place("seven", up) & straight(up) & has_next
 
+    first_duals = (cross_up & is_odd) | (cross_dn & is_even)
+
     def sends_dual(up):
         return (cross_up if up else cross_dn) & jnp.logical_not(straight(up)) & has_prev
-
-    loads = [
-        pltpu.make_async_copy(src, dst, load_sem.at[at])
-        for at, (src, dst) in enumerate(
-            (
-                (lam_hbm, lam),
-                (spread_hbm, spread),
-                (incr_hbm, incr),
-                (winds_hbm, w3.at[1]),
-                (members_hbm, members),
-                (mixing_hbm, mixing),
-                (vert_hbm, vert),
-            )
-        )
-    ]
-    for load in loads:
-        load.start()
 
     barrier = pltpu.get_barrier_semaphore()
     greetings = [
@@ -135,6 +120,23 @@
         def _():
             pl.semaphore_signal(barrier, inc=1, device_id=where, device_id_type=MESH)
 
+    loads = [
+        pltpu.make_async_copy(src, dst, load_sem.at[at])
+        for at, (src, dst) in enumerate(
+            (
+                (lam_hbm, lam),
+                (spread_hbm, spread),
+                (incr_hbm, incr),
+                (winds_hbm, w3.at[1]),
+                (members_hbm, members),
+                (mixing_hbm, mixing),
+                (vert_hbm, vert),
+            )
+        )
+    ]
+    for load in loads:
+        load.start()
+
     def ends(item, up):
         if item == WIN:
             return w3.at[1], w3.at[0 if up else 2]
@@ -301,9 +303,11 @@
 
     for load in loads[4:]:
         load.wait()
-    for base, matrix in ((0, mixing[...]), (4, vert[...])):
-        mats[base], mats[base + 1] = split(matrix)
-        mats[base + 2], mats[base + 3] = split(matrix.T)
+    mats[0], mats[1] = split(mixing[...])
+    mats[2], mats[3] = split(mixing[...].T)
+    high, low = split(vert[...])
+    high_t, low_t = split(vert[...].T)
+    mats[4], mats[5] = split(dot(high, high_t) + (dot(high, low_t) + dot(low, high_t)))
 
     for at, size in CHUNKS:
         rows = pl.ds(at, size)
@@ -318,24 +322,22 @@
                 term = perturb[row] * (weighted[row] + 0.25 * near)
                 totals[row] = term if m == 0 else totals[row] + term
         for row in range(2):
-            ens[row, rows, :] = totals[row]
+            ens[row, rows, :] = (0.5 / (NENS - 1)) * totals[row] + incr[row, rows, :]
 
     edges = [QEN + m for m in range(NENS)]
     start_lat(edges, sides=(True,))
     start_lat(edges[:2], sides=(False,))
-    def dual_row(row):
-        @pl.when(has_next)
+    def dual_row(row, cond=True):
+        @pl.when(has_next & cond)
         def _():
             dual_to_prev(row).wait_recv()
 
-        start_lat([LNX + row], has_next)
-
-    pass_on([SCA, SCA + 1])
+        start_lat([LNX + row], has_next & cond)
+
+    pass_on([SCA, SCA + 1], ("seven",))
     pass_duals()
-    dual_row(0)
-    pass_on(edges, ("six",))
-    dual_row(1)
-    start_lat(edges[2:], sides=(False,))
+    for row in range(2):
+        dual_row(row, first_duals)
 
     def weights(i):
         block, row = (i + 2) // 2, (i + 2) % 2
@@ -381,7 +383,35 @@
             prop_send[i] = product(mats, 0, za[i]).astype(BF16)
             prop_to_next(i).start()
 
+    dual_row(0, jnp.logical_not(first_duals))
+    pass_on(edges, ("six",))
+    dual_row(1, jnp.logical_not(first_duals))
+    start_lat(edges[2:], sides=(False,))
+    pass_on([SCA, SCA + 1], ("one",))
     pass_on(edges, ("seven", "one"))
+
+    early_edges = cross_up & is_even
+
+    def add_edges(cond):
+        await_lat(edges, cond)
+
+        @pl.when(cond)
+        def _():
+            for i in range(2):
+                for at, size in CHUNKS:
+                    rows = pl.ds(at, size)
+                    near = None
+                    for m in range(NENS):
+                        term = members[i, m, rows, :].astype(F32) * q_recv[i, m, rows, :].astype(F32)
+                        near = term if m == 0 else near + term
+                    ens[i, rows, :] += (0.5 * 0.25 / (NENS - 1)) * near
+
+    @pl.when(has_next)
+    def _():
+        for i in (2, 3):
+            ya[i] = product_16(mats, 2, l6[i])
+
+    add_edges(early_edges)
 
     await_lat([SCA, SCA + 1])
 
@@ -403,17 +433,10 @@
             rows = pl.ds(at, size)
             zb[i, rows, :] = smooth(lambda j, r: za[j + 1, r, :], i, rows)
     for i in range(2):
-        za[i] = product(mats, 6, zb[i])
-    for i in range(2):
-        zb[i] = product(mats, 4, za[i])
-    for i in range(2):
+        za[i] = product(mats, 4, zb[i])
         for at, size in CHUNKS:
             rows = pl.ds(at, size)
-            ens[i, rows, :] = (
-                0.5 * (spread[i, rows, :] * zb[i, rows, :])
-                + (0.5 / (NENS - 1)) * ens[i, rows, :]
-                + incr[i, rows, :]
-            )
+            ens[i, rows, :] += 0.5 * (spread[i, rows, :] * za[i, rows, :])
 
     @pl.when(has_next)
     def _():
@@ -426,13 +449,13 @@
             total = centre * here + north * of(i - 1, rows) + south * of(i + 1, rows)
             return total + west_of(east * here) + east_of(west * here)
 
-        for i in range(6):
-            zb[i] = product_16(mats, 2, l6[i])
+        for i in (0, 1, 4, 5):
+            ya[i] = product_16(mats, 2, l6[i])
         for i in range(-1, 3):
             for at, size in CHUNKS:
                 rows = pl.ds(at, size)
                 za[i + 1, rows, :] = inside(
-                    i, transport_back(lambda j, r: zb[j + 2, r, :], i, rows)
+                    i, transport_back(lambda j, r: ya[j + 2, r, :], i, rows)
                 )
         for i in range(4):
             zb[i] = product(mats, 2, za[i])
@@ -446,7 +469,7 @@
     def _():
         incr_out[...] = lam[...]
 
-    await_lat(edges)
+    add_edges(jnp.logical_not(early_edges))
 
     @pl.when(has_prev)
     def _():
@@ -463,15 +486,7 @@
     for i in range(2):
         for at, size in CHUNKS:
             rows = pl.ds(at, size)
-            near = None
-            for m in range(NENS):
-                term = members[i, m, rows, :].astype(F32) * q_recv[i, m, rows, :].astype(F32)
-                near = term if m == 0 else near + term
-            lam_out[i, rows, :] = (
-                ens[i, rows, :]
-                + (0.5 * 0.25 / (NENS - 1)) * near
-                - arrived[i, rows, :].astype(F32)
-            )
+            lam_out[i, rows, :] = ens[i, rows, :] - arrived[i, rows, :].astype(F32)
 
     @pl.when(has_prev)
     def _():
@@ -540,10 +555,11 @@
         pltpu.VMEM((2, *row), BF16),
         pltpu.VMEM((2, *row), BF16),
         pltpu.VMEM((SLOTS, *row), BF16),
-        pltpu.VMEM((8, COMP, COMP), BF16),
+        pltpu.VMEM((6, COMP, COMP), BF16),
         pltpu.VMEM((2, *row), F32),
+        pltpu.VMEM((6, *row), F32),
         pltpu.VMEM((4, *row), F32),
-        pltpu.VMEM((6, *row), F32),
+        pltpu.VMEM((4, *row), F32),
         pltpu.VMEM((2, *row), F32),
         dma((7,)),
         dma((4,)),

time: 29.4 us -> 29.4 us (level)
  no operation moved by 1% of the time
where the time goes in v5:
time: 29.4 us; the launch traced here: 29.3 us
  Pallas kernels  27.1 us (92%)
  local copies, waits for them, and re-layouts  1.53 us (5%)
  between operations  0.64 us (2%)
    pallas_call x1, Pallas kernels, per_device(): pl.pallas_call(kernel, out_shape=(state, state), in_specs=[pl.BlockSpec(m...  27.1 us
    unnamed x2, local copies, waits for them, and re-layouts  1.53 us

profile of v5, /device:TPU:390, one launch (start us, length us, event | category | flops | bytes accessed | tf_op | source)
XLA Modules:
  0.0 29.3 jit_solution(3267435205288129884)
XLA Ops:
  0.6 27.1 %shard_map.86 = (f32[2,216,256]{2,1,0:T(8,128)S(1)}, f32[2,216,256]{2,1,0:T(8,128)S(1)}) custom-call(f32[2,216,256]{2,1,0:T(8,128)} %bitcast.11, f32[2,216,256]{2,1,0:T(8,128)} %bitcast.12, f32[4,2,256]{2,1,0:T(2,128)} %bitcast.15, f32[216,216]{1,0:T(8,128)} %bitcast.14, f32[2,216,256]{2,1,0:T(8,128)} %bitcast.13, f32[216,216]{1,0:T(8,128)} %vert_hbm.1, ...), custom_call_target="tpu_custom_call" | custom-call | tf_op jit(solution)/shard_map/pallas_call | solution.py:575
  27.7 0.8 %copy.11 = f32[1,2,216,256]{3,2,1,0:T(8,128)} copy(f32[1,2,216,256]{3,2,1,0:T(8,128)S(1)} %bitcast.9) | data formatting | bytes 884736
  28.5 0.8 %copy.12 = f32[1,2,216,256]{3,2,1,0:T(8,128)} copy(f32[1,2,216,256]{3,2,1,0:T(8,128)S(1)} %bitcast.8) | data formatting | bytes 884736

commit v6 on v5

--- a/solution.py
+++ b/solution.py
@@ -8,15 +8,16 @@
 MESH = pl.DeviceIdType.MESH
 F32, BF16 = jnp.float32, jnp.bfloat16
 COMP, LON, NENS = 216, 256, 4
+HALF = LON // 2
 TM, LAT, BAND = 8, 64, 16
 CHUNKS = [(at, min(32, COMP - at)) for at in range(0, COMP, 32)]
 
-WIN, INC, SCA, LNX, QEN = 0, 1, 3, 5, 7
+WIN, INC, SCA, LNX, MEM, DUAL, BACK = 0, 1, 3, 5, 7, 9, 10
 ITEMS = 11
 PLACES = {"seven": 14, "six": 12, "one": 2}
 ROUTES = {
-    True: {"seven": (SCA, SCA + 1, QEN), "six": (QEN + 2, QEN + 3)},
-    False: {"seven": (QEN, QEN + 1), "one": (SCA, SCA + 1, QEN + 2, QEN + 3)},
+    True: {"seven": (SCA, SCA + 1, MEM), "six": (MEM + 1, DUAL)},
+    False: {"seven": (MEM,), "one": (SCA, SCA + 1, MEM + 1, DUAL)},
 }
 RELAYS = [(kind, even) for even, kinds in ROUTES.items() for kind in kinds]
 FAR = 4
@@ -59,7 +60,7 @@
 def kernel(
     lam_hbm, incr_hbm, winds_hbm, mixing_hbm, spread_hbm, vert_hbm, members_hbm, lam_out, incr_out,
     lam, incr, mixing, spread, vert, members,
-    i6, l6, s6, w3, q_send, q_recv, lam_send, prop_send, arrived, fwd,
+    i6, l6, s6, w3, p_recv, d_recv, b_send, b_recv, lam_send, prop_send, arrived, fwd, fwd_p, fwd_d,
     mats, scaled, ya, za, zb, ens,
     load_sem, tm_send, tm_recv, up_send, up_recv, dn_send, dn_recv, f_in, f_out, far_send,
 ):
@@ -144,8 +145,18 @@
             if first <= item < first + 2:
                 row = item - first
                 return buffer.at[2 + row], buffer.at[row if up else 4 + row]
-        m = item - QEN
-        return q_send.at[1 if up else 0, m], q_recv.at[0 if up else 1, m]
+        row, side, half = (1, 0, pl.ds(0, HALF)) if up else (0, 1, pl.ds(HALF, HALF))
+        if item == DUAL:
+            return lam_send.at[row, :, half], d_recv.at[side]
+        if item == BACK:
+            return b_send.at[row], b_recv.at[side]
+        pair = pl.ds(2 * (item - MEM), 2)
+        return members.at[row, pair, :, half], p_recv.at[side, pair]
+
+    def slot(item, at):
+        if item in (MEM, MEM + 1):
+            return fwd_p.at[item - MEM]
+        return fwd_d if item == DUAL else fwd.at[at]
 
     def to_lat(item, up):
         src, dst = ends(item, up)
@@ -169,7 +180,7 @@
         p = PLACES[kind]
         where = {"lat": lat + p + 1 if up else lat - p - 1}
         return pltpu.make_async_remote_copy(
-            src, fwd.at[at], send.at[item], f_in.at[at], device_id=where, device_id_type=MESH
+            src, slot(item, at), send.at[item], f_in.at[at], device_id=where, device_id_type=MESH
         )
 
     def from_fwd(item, kind, at, up):
@@ -178,7 +189,7 @@
         p = PLACES[kind]
         where = {"lat": lat - p if up else lat + p}
         return pltpu.make_async_remote_copy(
-            fwd.at[at], dst, f_out.at[at], recv.at[item], device_id=where, device_id_type=MESH
+            slot(item, at), dst, f_out.at[at], recv.at[item], device_id=where, device_id_type=MESH
         )
 
     def start_lat(items, cond=True, sides=(True, False)):
@@ -204,14 +215,14 @@
 
     def hand_over(item, kind, at, up):
         pltpu.make_async_remote_copy(
-            fwd.at[at], fwd.at[at], f_out.at[at], f_in.at[at],
+            slot(item, at), slot(item, at), f_out.at[at], f_in.at[at],
             device_id={"lat": lat - 1 if up else lat + 1}, device_id_type=MESH,
         ).wait_recv()
         from_fwd(item, kind, at, up).start()
 
-    def pass_on(items, kinds=tuple(PLACES)):
+    def pass_on(items, kinds, parities=(True, False)):
         for kind, even in RELAYS:
-            if kind not in kinds:
+            if kind not in kinds or even not in parities:
                 continue
             now = [item for item in items if item in ROUTES[even][kind]]
             if not now:
@@ -269,8 +280,6 @@
         for buffer in (i6, l6, s6):
             for row in (0, 1):
                 buffer[row] = jnp.zeros_like(buffer[row])
-        for m in range(NENS):
-            q_recv[0, m] = jnp.zeros_like(q_recv[0, m])
 
     @pl.when(jnp.logical_not(has_up))
     def _():
@@ -278,8 +287,6 @@
         for buffer in (i6, l6, s6):
             for row in (4, 5):
                 buffer[row] = jnp.zeros_like(buffer[row])
-        for m in range(NENS):
-            q_recv[1, m] = jnp.zeros_like(q_recv[1, m])
 
     @pl.when(jnp.logical_not(has_prev))
     def _():
@@ -293,6 +300,9 @@
         dual_to_prev(1).start()
 
     start_lat([WIN, INC, INC + 1], has_next)
+    loads[4].wait()
+    edges = [MEM, MEM + 1, DUAL]
+    start_lat(edges, sides=(True,))
     start_lat([SCA, SCA + 1])
     for up in (True, False):
 
@@ -301,7 +311,7 @@
             for row in range(2):
                 dual_across(row, up).start()
 
-    for load in loads[4:]:
+    for load in loads[5:]:
         load.wait()
     mats[0], mats[1] = split(mixing[...])
     mats[2], mats[3] = split(mixing[...].T)
@@ -317,16 +327,13 @@
             perturb = [members[row, m, rows, :].astype(F32) for row in range(2)]
             weighted = [perturb[row] * duals[row] for row in range(2)]
             for row in range(2):
-                q_send[row, m, rows, :] = weighted[row].astype(BF16)
                 near = weighted[1 - row] + east_of(weighted[row]) + west_of(weighted[row])
                 term = perturb[row] * (weighted[row] + 0.25 * near)
                 totals[row] = term if m == 0 else totals[row] + term
         for row in range(2):
             ens[row, rows, :] = (0.5 / (NENS - 1)) * totals[row] + incr[row, rows, :]
 
-    edges = [QEN + m for m in range(NENS)]
-    start_lat(edges, sides=(True,))
-    start_lat(edges[:2], sides=(False,))
+    start_lat(edges, sides=(False,))
     def dual_row(row, cond=True):
         @pl.when(has_next & cond)
         def _():
@@ -334,6 +341,7 @@
 
         start_lat([LNX + row], has_next & cond)
 
+    pass_on(edges, ("seven",), (True,))
     pass_on([SCA, SCA + 1], ("seven",))
     pass_duals()
     for row in range(2):
@@ -383,35 +391,54 @@
             prop_send[i] = product(mats, 0, za[i]).astype(BF16)
             prop_to_next(i).start()
 
+    pass_on(edges, ("six",))
     dual_row(0, jnp.logical_not(first_duals))
-    pass_on(edges, ("six",))
+    pass_on(edges, ("one",))
+    pass_on([SCA, SCA + 1], ("one",))
     dual_row(1, jnp.logical_not(first_duals))
-    start_lat(edges[2:], sides=(False,))
-    pass_on([SCA, SCA + 1], ("one",))
-    pass_on(edges, ("seven", "one"))
-
-    early_edges = cross_up & is_even
-
-    def add_edges(cond):
-        await_lat(edges, cond)
-
-        @pl.when(cond)
-        def _():
-            for i in range(2):
+    pass_on(edges, ("seven",), (False,))
+
+    scale = 0.5 * 0.25 / (NENS - 1)
+
+    def edge_products(from_below, cond):
+        has = (has_dn if from_below else has_up) & cond
+        row, side, half = (0, 0, pl.ds(0, HALF)) if from_below else (1, 1, pl.ds(HALF, HALF))
+
+        @pl.when(has)
+        def _():
+            for item in edges:
+                to_lat(item, from_below).wait_recv()
+            for at, size in CHUNKS:
+                rows = pl.ds(at, size)
+                both = None
+                for m in range(NENS):
+                    term = members[row, m, rows, half].astype(F32) * p_recv[side, m, rows, :].astype(F32)
+                    both = term if m == 0 else both + term
+                ens[row, rows, half] += scale * (both * d_recv[side, rows, :].astype(F32))
+                b_send[row, rows, :] = (both * lam[row, rows, half]).astype(BF16)
+            to_lat(BACK, not from_below).start()
+
+    def add_back():
+        await_lat([BACK])
+        for from_below, has in ((True, has_dn), (False, has_up)):
+            row, side, half = (0, 0, pl.ds(HALF, HALF)) if from_below else (1, 1, pl.ds(0, HALF))
+
+            @pl.when(has)
+            def _():
                 for at, size in CHUNKS:
                     rows = pl.ds(at, size)
-                    near = None
-                    for m in range(NENS):
-                        term = members[i, m, rows, :].astype(F32) * q_recv[i, m, rows, :].astype(F32)
-                        near = term if m == 0 else near + term
-                    ens[i, rows, :] += (0.5 * 0.25 / (NENS - 1)) * near
+                    ens[row, rows, half] += scale * b_recv[side, rows, :].astype(F32)
+
+    edge_products(True, jnp.logical_not(cross_dn))
+    edge_products(False, jnp.logical_not(cross_up))
 
     @pl.when(has_next)
     def _():
         for i in (2, 3):
             ya[i] = product_16(mats, 2, l6[i])
 
-    add_edges(early_edges)
+    edge_products(True, cross_dn)
+    edge_products(False, cross_up)
 
     await_lat([SCA, SCA + 1])
 
@@ -469,7 +496,7 @@
     def _():
         incr_out[...] = lam[...]
 
-    add_edges(jnp.logical_not(early_edges))
+    add_back()
 
     @pl.when(has_prev)
     def _():
@@ -502,7 +529,7 @@
 
         @pl.when(has)
         def _():
-            for item in [SCA, SCA + 1, *edges]:
+            for item in [SCA, SCA + 1, *edges, BACK]:
                 to_lat(item, up).wait_send()
 
         @pl.when(has & has_next)
@@ -549,12 +576,16 @@
         pltpu.VMEM((6, *row), BF16),
         pltpu.VMEM((6, *row), BF16),
         pltpu.VMEM((3, 4, 2, LON), F32),
-        pltpu.VMEM((2, NENS, *row), BF16),
-        pltpu.VMEM((2, NENS, *row), BF16),
+        pltpu.VMEM((2, NENS, COMP, HALF), BF16),
+        pltpu.VMEM((2, COMP, HALF), BF16),
+        pltpu.VMEM((2, COMP, HALF), BF16),
+        pltpu.VMEM((2, COMP, HALF), BF16),
         pltpu.VMEM((2, *row), BF16),
         pltpu.VMEM((2, *row), BF16),
         pltpu.VMEM((2, *row), BF16),
         pltpu.VMEM((SLOTS, *row), BF16),
+        pltpu.VMEM((2, 2, COMP, HALF), BF16),
+        pltpu.VMEM((COMP, HALF), BF16),
         pltpu.VMEM((6, COMP, COMP), BF16),
         pltpu.VMEM((2, *row), F32),
         pltpu.VMEM((6, *row), F32),

time: 29.4 us -> 29 us (0.986)
  the two profiles are of different devices: /device:TPU:390 before, /device:TPU:189 now
where the time goes in v6:
time: 29 us; the launch traced here: 28.9 us
  Pallas kernels  26.7 us (92%)
  local copies, waits for them, and re-layouts  1.53 us (5%)
  between operations  0.64 us (2%)
    pallas_call x1, Pallas kernels, per_device(): pl.pallas_call(kernel, out_shape=(state, state), in_specs=[pl.BlockSpec(m...  26.7 us
    unnamed x2, local copies, waits for them, and re-layouts  1.53 us

profile of v6, /device:TPU:189, one launch (start us, length us, event | category | flops | bytes accessed | tf_op | source)
XLA Modules:
  0.0 28.9 jit_solution(16929654671825838174)
XLA Ops:
  0.6 26.7 %shard_map.86 = (f32[2,216,256]{2,1,0:T(8,128)S(1)}, f32[2,216,256]{2,1,0:T(8,128)S(1)}) custom-call(f32[2,216,256]{2,1,0:T(8,128)} %bitcast.11, f32[2,216,256]{2,1,0:T(8,128)} %bitcast.12, f32[4,2,256]{2,1,0:T(2,128)} %bitcast.15, f32[216,216]{1,0:T(8,128)} %bitcast.14, f32[2,216,256]{2,1,0:T(8,128)} %bitcast.13, f32[216,216]{1,0:T(8,128)} %vert_hbm.1, ...), custom_call_target="tpu_custom_call" | custom-call | tf_op jit(solution)/shard_map/pallas_call | solution.py:606
  27.4 0.8 %copy.11 = f32[1,2,216,256]{3,2,1,0:T(8,128)} copy(f32[1,2,216,256]{3,2,1,0:T(8,128)S(1)} %bitcast.9) | data formatting | bytes 884736
  28.1 0.8 %copy.12 = f32[1,2,216,256]{3,2,1,0:T(8,128)} copy(f32[1,2,216,256]{3,2,1,0:T(8,128)S(1)} %bitcast.8) | data formatting | bytes 884736

commit v7 on v6

--- a/solution.py
+++ b/solution.py
@@ -16,7 +16,7 @@
 ITEMS = 11
 PLACES = {"seven": 14, "six": 12, "one": 2}
 ROUTES = {
-    True: {"seven": (SCA, SCA + 1, MEM), "six": (MEM + 1, DUAL)},
+    True: {"seven": (SCA, MEM), "six": (SCA + 1, MEM + 1, DUAL)},
     False: {"seven": (MEM,), "one": (SCA, SCA + 1, MEM + 1, DUAL)},
 }
 RELAYS = [(kind, even) for even, kinds in ROUTES.items() for kind in kinds]
@@ -342,8 +342,8 @@
         start_lat([LNX + row], has_next & cond)
 
     pass_on(edges, ("seven",), (True,))
+    pass_duals()
     pass_on([SCA, SCA + 1], ("seven",))
-    pass_duals()
     for row in range(2):
         dual_row(row, first_duals)
 
@@ -392,6 +392,7 @@
             prop_to_next(i).start()
 
     pass_on(edges, ("six",))
+    pass_on([SCA + 1], ("six",))
     dual_row(0, jnp.logical_not(first_duals))
     pass_on(edges, ("one",))
     pass_on([SCA, SCA + 1], ("one",))

time: 29 us -> 29 us (level)
  no operation moved by 1% of the time
where the time goes in v7:
time: 29 us; the launch traced here: 28.8 us
  Pallas kernels  26.7 us (92%)
  local copies, waits for them, and re-layouts  1.53 us (5%)
  between operations  0.64 us (2%)
    pallas_call x1, Pallas kernels, per_device(): pl.pallas_call(kernel, out_shape=(state, state), in_specs=[pl.BlockSpec(m...  26.7 us
    unnamed x2, local copies, waits for them, and re-layouts  1.53 us

profile of v7, /device:TPU:189, one launch (start us, length us, event | category | flops | bytes accessed | tf_op | source)
XLA Modules:
  0.0 28.8 jit_solution(4941303889683238973)
XLA Ops:
  0.6 26.7 %shard_map.86 = (f32[2,216,256]{2,1,0:T(8,128)S(1)}, f32[2,216,256]{2,1,0:T(8,128)S(1)}) custom-call(f32[2,216,256]{2,1,0:T(8,128)} %bitcast.11, f32[2,216,256]{2,1,0:T(8,128)} %bitcast.12, f32[4,2,256]{2,1,0:T(2,128)} %bitcast.15, f32[216,216]{1,0:T(8,128)} %bitcast.14, f32[2,216,256]{2,1,0:T(8,128)} %bitcast.13, f32[216,216]{1,0:T(8,128)} %vert_hbm.1, ...), custom_call_target="tpu_custom_call" | custom-call | tf_op jit(solution)/shard_map/pallas_call | solution.py:607
  27.3 0.8 %copy.11 = f32[1,2,216,256]{3,2,1,0:T(8,128)} copy(f32[1,2,216,256]{3,2,1,0:T(8,128)S(1)} %bitcast.9) | data formatting | bytes 884736
  28.1 0.8 %copy.12 = f32[1,2,216,256]{3,2,1,0:T(8,128)} copy(f32[1,2,216,256]{3,2,1,0:T(8,128)S(1)} %bitcast.8) | data formatting | bytes 884736
